TPU v7x, 512 devices: a whole 4x4x16 slice. The times are simulated.
512 devices in a mesh: seq: 32 (over x, z_lo), pass: 2 (over core), head: 8 (over z_hi, y).
Axes of the slice: x: 4, y: 4, z: 16 (z_hi: 2, z_lo: 8; z = z_hi * 8 + z_lo), core: 2. Of those that a mesh axis runs over, the one named last changes fastest.
Arguments:
- queries: bfloat16 [2, 4096, 3072], P('pass', 'seq', 'head'), may hold values from -8 to 8
- keys: bfloat16 [2, 4096, 3072], P('pass', 'seq', 'head'), may hold values from -8 to 8
- values: bfloat16 [2, 4096, 3072], P('pass', 'seq', 'head'), may hold values from -6 to 6
- self_pairs: int32 [2, 160, 2], replicated, may hold values from 0 to 31, as said below
- mask_pairs: int32 [128, 2], replicated, may hold values from 0 to 31, as said below
- counts: int32 [3], replicated, may hold values from 32 to 160, as said below
- out_weight: bfloat16 [3072, 3072], P('head'), may hold values from -0.109375 to 0.109375
Outputs:
- projected: bfloat16 [2, 4096, 3072], P('pass', 'seq', 'head')
Inputs may be any that keep to these rules, and one draw needn't show every extreme that they name: `self_pairs`: tile numbers. In each pass's list the first 32 entries are (t, t) for t = 0 to 31; the first counts[p] entries are live, the rest are padding; pairs may repeat. `mask_pairs`: tile numbers; the first counts[2] entries are live; pairs may repeat. counts[0] and counts[1] lie between 32 and 160, and one of them is 160; counts[2] lies between 64 and 128.
All inputs are finite; a program needn't handle non-finite values.
Results may differ from a plain program's by a relative error of at most 0.01.
Values may be sent and summed in bfloat16 or wider, within the bound.
A program may use at most 64 MiB of HBM per device.

v0:
```python
import jax
import jax.numpy as jnp
from jax import lax
from jax.sharding import PartitionSpec as P

HD = 128
TILE = 128


NEG_FILL = -1e30


def broadcast(value, axis, source):
    kept = jnp.where(lax.axis_index(axis) == source, value, 0).astype(value.dtype)
    return lax.psum(kept, axis)


def local_table(pairs, live_count, first_tile, query_tiles, total_tiles):
    entries = jnp.arange(pairs.shape[0], dtype=jnp.int32)
    live = entries < live_count
    mine = first_tile + jnp.arange(query_tiles, dtype=jnp.int32)
    row_hits = ((pairs[:, 0][:, None] == mine[None, :]) & live[:, None]).astype(jnp.float32)
    col_hits = (pairs[:, 1][:, None] == jnp.arange(total_tiles, dtype=jnp.int32)[None, :]).astype(
        jnp.float32
    )
    return jnp.dot(row_hits.T, col_hits) > 0.5


def empty_state(query_tiles, head_count):
    running_max = jnp.full((query_tiles, head_count, TILE), NEG_FILL, jnp.float32)
    running_total = jnp.zeros((query_tiles, head_count, TILE), jnp.float32)
    running_acc = jnp.zeros((query_tiles, TILE, head_count, HD), jnp.float32)
    return (running_max, running_total, running_acc)


def absorb_block(single, query_block, key_tile, value_tile, allowed):

    def include(current):
        old_max, old_total, old_acc = current
        scores = jnp.einsum(
            "qhd,khd->hqk", query_block, key_tile, preferred_element_type=jnp.float32
        ) * HD ** (-0.5)
        new_max = jnp.maximum(old_max, jnp.max(scores, axis=2))
        exps = jnp.exp(scores - new_max[:, :, None])
        faded = jnp.exp(old_max - new_max)
        new_total = old_total * faded + jnp.sum(exps, axis=2)
        weights = exps.astype(jnp.bfloat16)
        gained = jnp.einsum("hqk,khd->qhd", weights, value_tile, preferred_element_type=jnp.float32)
        new_acc = old_acc * faded.T[:, :, None] + gained
        return (new_max, new_total, new_acc)

    def unchanged(current):
        return current

    return lax.cond(allowed, include, unchanged, single)


def pick_tile(carried, position):
    return tuple((member[position] for member in carried))


def store_tile(carried, position, single):
    return tuple((member.at[position].set(fresh) for member, fresh in zip(carried, single)))


def on_device(queries, keys, values, self_pairs, mask_pairs, counts, out_weight):
    pass_index = lax.axis_index("pass")
    seq_index = lax.axis_index("seq")
    is_edit = pass_index == 1
    tok_dev = queries.shape[1]
    row_width = queries.shape[2]
    head_count = row_width // HD
    query_tiles = tok_dev // TILE
    total_tiles = lax.axis_size("seq") * query_tiles
    query_rows = queries[0]
    key_rows = keys[0]
    value_rows = values[0]
    query_blocks = query_rows.reshape(query_tiles, TILE, head_count, HD)
    first_tile = seq_index * query_tiles
    own_pairs = lax.dynamic_index_in_dim(self_pairs, pass_index, 0, keepdims=False)
    own_count = lax.dynamic_index_in_dim(counts, pass_index, 0, keepdims=False)
    self_table = local_table(own_pairs, own_count, first_tile, query_tiles, total_tiles)
    cross_table = local_table(mask_pairs, counts[2], first_tile, query_tiles, total_tiles)

    def tile_of(rows, offset):
        return lax.dynamic_slice_in_dim(rows, offset * TILE, TILE, 0).reshape(TILE, head_count, HD)

    source_key_rows, source_value_rows = (
        broadcast(key_rows, "pass", 0),
        broadcast(value_rows, "pass", 0),
    )
    own_keys = lax.all_gather(key_rows, "seq", axis=0, tiled=True)
    own_values = lax.all_gather(value_rows, "seq", axis=0, tiled=True)
    far_keys = lax.all_gather(source_key_rows, "seq", axis=0, tiled=True)
    far_values = lax.all_gather(source_value_rows, "seq", axis=0, tiled=True)

    def visit(offset, current):
        key_tile = tile_of(own_keys, offset)
        value_tile = tile_of(own_values, offset)
        far_key_tile = tile_of(far_keys, offset)
        far_value_tile = tile_of(far_values, offset)
        single = pick_tile(current, 0)
        single = absorb_block(single, query_blocks[0], key_tile, value_tile, self_table[0, offset])
        single = absorb_block(
            single, query_blocks[0], far_key_tile, far_value_tile, cross_table[0, offset] & is_edit
        )
        current = store_tile(current, 0, single)
        return current

    final_state = lax.fori_loop(
        0, own_keys.shape[0] // TILE, visit, empty_state(query_tiles, head_count)
    )
    final_max, final_total, final_acc = final_state
    normalized = final_acc / jnp.swapaxes(final_total, 1, 2)[..., None]
    attended = normalized.reshape(tok_dev, row_width).astype(jnp.bfloat16)
    partial_sums = jnp.dot(attended, out_weight, preferred_element_type=jnp.float32)
    summed = lax.psum_scatter(partial_sums, "head", scatter_dimension=1, tiled=True)
    return summed.astype(jnp.bfloat16)[None]


def solution(mesh):
    in_specs = (
        P("pass", "seq", "head"),
        P("pass", "seq", "head"),
        P("pass", "seq", "head"),
        P(),
        P(),
        P(),
        P("head", None),
    )
    out_specs = P("pass", "seq", "head")
    return jax.shard_map(
        on_device, mesh=mesh, in_specs=in_specs, out_specs=out_specs, check_vma=False
    )
```

profile of v0, /device:TPU:4, one launch (start us, length us, event | category | flops | bytes accessed | tf_op | source)
XLA Modules:
  0.0 1092.5 jit_solution(15133535653517579764)
XLA Ops:
  7.4 1.2 copy.18
  8.5 1.0 copy.19
  12.2 42.6 %all-reduce.3.cloned.1.call-done = (bf16[128,384]{0,1:T(8,128)(2,1)}, bf16[128,384]{0,1:T(8,128)(2,1)}) async-done(((bf16[128,384]{0,1:T(8,128)(2,1)}, bf16[128,384]{0,1:T(8,128)(2,1)}), (bf16[128,384]{0,1:T(8,128)(2,1)}, bf16[128,384]{0,1:T(8,128)(2,1)})) %all-reduce.3.cloned.1.call-update) | async-done | bytes 196624 | tf_op jit(solution)/shard_map/psum | solution.py:15
  56.3 1.0 copy.22
  57.3 1.3 fusion.33
  59.3 1.5 fusion.15
  61.6 144.3 %all-gather.11.cloned.1.call-done = bf16[1,4096,384]{1,2,0:T(8,128)(2,1)} async-done(((bf16[1,128,384]{1,2,0:T(8,128)(2,1)}), bf16[1,4096,384]{1,2,0:T(8,128)(2,1)}) %all-gather.11.cloned.1.call-update) | async-done | bytes 3145744 | tf_op jit(solution)/shard_map/all_gather | solution.py:92
  205.9 197.6 %all-gather.13.cloned.1.call-done = bf16[1,4096,384]{1,2,0:T(8,128)(2,1)} async-done(((bf16[1,128,384]{1,2,0:T(8,128)(2,1)}), bf16[1,4096,384]{1,2,0:T(8,128)(2,1)}) %all-gather.13.cloned.1.call-update) | async-done | bytes 3145744 | tf_op jit(solution)/shard_map/all_gather | solution.py:93
  403.5 197.2 %all-gather.7.cloned.1.call-done = bf16[4096,384]{0,1:T(8,128)(2,1)} async-done(((bf16[128,384]{0,1:T(8,128)(2,1)}), bf16[4096,384]{0,1:T(8,128)(2,1)}) %all-gather.7.cloned.1.call-update) | async-done | bytes 3145744 | tf_op jit(solution)/shard_map/all_gather | solution.py:94
  600.7 197.3 %all-gather.9.cloned.1.call-done = bf16[4096,384]{0,1:T(8,128)(2,1)} async-done(((bf16[128,384]{0,1:T(8,128)(2,1)}), bf16[4096,384]{0,1:T(8,128)(2,1)}) %all-gather.9.cloned.1.call-update) | async-done | bytes 3145744 | tf_op jit(solution)/shard_map/all_gather | solution.py:95
  798.7 113.6 %while.23 = (s32[]{:T(128)}, f32[1,3,128]{2,1,0:T(4,128)}, f32[1,3,128]{2,1,0:T(4,128)S(1)}, f32[1,128,3,128]{3,1,2,0:T(8,128)S(1)}, pred[1,32]{1,0:T(4,128)(4,1...) while((s32[]{:T(128)}, f32[1,3,128]{2,1,0:T(4,128)}, ...), condition=%wide.region_11.12_spmd, body=%wide.region_2.11_spmd.sunk | while | flops 51120392 | bytes 3391902 | solution.py:110
  799.9 1.0 constant_dynamic-slice_fusion.9
  803.4 1.0 constant_dynamic-slice_fusion.9
  806.8 1.0 constant_dynamic-slice_fusion.9
  810.3 1.0 constant_dynamic-slice_fusion.9
  813.8 1.0 constant_dynamic-slice_fusion.9
  817.3 1.0 constant_dynamic-slice_fusion.9
  820.7 1.0 constant_dynamic-slice_fusion.9
  824.2 1.0 constant_dynamic-slice_fusion.9
  827.7 1.0 constant_dynamic-slice_fusion.9
  831.1 1.0 constant_dynamic-slice_fusion.9
  834.6 1.0 constant_dynamic-slice_fusion.9
  838.1 1.0 constant_dynamic-slice_fusion.9
  841.6 1.0 constant_dynamic-slice_fusion.9
  855.4 1.0 constant_dynamic-slice_fusion.9
  856.4 3.1 conditional.4
  864.9 1.0 constant_dynamic-slice_fusion.9
  892.7 1.0 constant_dynamic-slice_fusion.9
  903.1 1.0 constant_dynamic-slice_fusion.9
  912.5 1.8 fusion.34
  914.3 169.1 %reduce-scatter.2.cloned.1.call-done = f32[128,384]{1,0:T(8,128)} async-done(((f32[128,3072]{1,0:T(8,128)}), f32[128,384]{1,0:T(8,128)}) %reduce-scatter.2.cloned.1.call-update) | async-done | bytes 196624 | tf_op jit(solution)/shard_map/reduce_scatter | solution.py:117
  1083.4 1.6 convert_bitcast_fusion
  (177 shorter events, 82.4 us)
Async XLA Ops:
  7.4 905.1 %copy-start = (bf16[384,3072]{1,0:T(8,128)(2,1)S(1)}, bf16[384,3072]{1,0:T(8,128)(2,1)}, u32[]{:S(2)}) copy-start(bf16[384,3072]{1,0:T(8,128)(2,1)} %param.25) | copy-start | bytes 7077892
  7.4 47.4 %all-reduce.3.cloned.1.call-start = ((), (), s32[]{:S(2)}) async-start(), calls=%async_computation.6 | async-start | bytes 393216 | tf_op jit(solution)/shard_map/psum | solution.py:15
  8.5 2.5 copy-start.2
  9.6 2.0 copy-start.1
  11.0 194.9 %all-gather.11.cloned.1.call-start = ((), (), s32[]{:S(2)}) async-start(), calls=%async_computation.4 | async-start | bytes 3244032 | tf_op jit(solution)/shard_map/all_gather | solution.py:92
  11.5 392.0 %all-gather.13.cloned.1.call-start = ((), (), s32[]{:S(2)}) async-start(), calls=%async_computation.5 | async-start | bytes 3244032 | tf_op jit(solution)/shard_map/all_gather | solution.py:93
  12.1 588.6 %all-gather.7.cloned.1.call-start = ((), (), s32[]{:S(2)}) async-start(), calls=%async_computation.1 | async-start | bytes 3244032 | tf_op jit(solution)/shard_map/all_gather | solution.py:94
  54.8 743.3 %all-gather.9.cloned.1.call-start = ((), (), s32[]{:S(2)}) async-start(), calls=%async_computation.2 | async-start | bytes 3244032 | tf_op jit(solution)/shard_map/all_gather | solution.py:95
  55.5 1027.8 %reduce-scatter.2.cloned.1.call-start = ((), (), s32[]{:S(2)}) async-start(), calls=%async_computation.3 | async-start | bytes 1769472 | tf_op jit(solution)/shard_map/reduce_scatter | solution.py:117
Sparse Core Ops, SparseCore 0:
  11.1 43.6 all-reduce.2
  914.4 168.8 reduce-scatter.1
Sparse Core Ops, SparseCore 1:
  13.4 192.4 all-gather.10
  207.8 195.7 all-gather.12
  405.4 195.3 all-gather.6
  602.7 195.3 all-gather.8
where the time goes:
time: 1100 us; the launch traced here: 1090 us
  waiting for transfers between devices  950 us (86%)
  local copies, waits for them, and re-layouts  60 us (5%)
  loops' own time  39.3 us (4%)
  other arithmetic  23.4 us (2%)
  between operations  15.1 us (1%)
    all_gather x1, waiting for transfers between devices, on_device(): own_values = lax.all_gather(value_rows, 'seq', axis=0, tiled=True)  198 us
    all_gather x1, waiting for transfers between devices, on_device(): far_values = lax.all_gather(source_value_rows, 'seq', axis=0, tiled=True)  197 us
    all_gather x1, waiting for transfers between devices, on_device(): far_keys = lax.all_gather(source_key_rows, 'seq', axis=0, tiled=True)  197 us
    reduce_scatter x1, waiting for transfers between devices, on_device(): lax.psum_scatter(partial_sums, 'head', scatter_dimension=1, tiled=True)  169 us
    all_gather x1, waiting for transfers between devices, on_device(): own_keys = lax.all_gather(key_rows, 'seq', axis=0, tiled=True)  144 us
    psum x1, waiting for transfers between devices, broadcast(): return lax.psum(kept, axis)  42.6 us
    dynamic_slice x32, local copies, waits for them, and re-layouts, tile_of(): lax.dynamic_slice_in_dim(rows, offset * TILE, TILE, 0)  30.9 us
  transfers between devices with their start and end apart: 6, of which 6 were waited for; matrix products, arithmetic and copies ran while one was open for 1% of the time, Pallas kernels for 0%

commit v1 on v0

v1 whole, which is shorter than its diff:
```python
import functools
import math

import jax
import jax.numpy as jnp
from jax import lax
from jax.experimental import pallas as pl
from jax.experimental.pallas import tpu as pltpu
from jax.sharding import PartitionSpec as P

HD = 128
TILE = 128
NX = 4
NZ = 8
NY = 4
NT = 32
SLOTS = 4
ENTRIES = 2 * NT
BF16 = jnp.bfloat16
F32 = jnp.float32
I32 = jnp.int32
EXP2_SCALE = HD ** -0.5 * math.log2(math.e)
MESH = pl.DeviceIdType.MESH


def head_of_row(z):
    return (3 * z + 1) // 8


def first_row(g):
    return (8 * g + 1) // 3


def last_row(g):
    return (8 * g + 9) // 3 - 1


def query_place(zq, g):
    if g == 0:
        return zq // 3, zq % 3
    if g == 1:
        return 3 + zq // 4, zq % 4
    return 7 - (7 - zq) // 3, (7 - zq) % 3


def slot_row(z, g, j):
    low = 3 * z + j
    mid = 4 * (z - 3) + j
    high = 7 - (3 * (7 - z) + j)
    row = jnp.where(g == 0, low, jnp.where(g == 1, mid, high))
    return jnp.where((j == 3) & (g != 1), -1, row)


def row_order(i, z):
    near = jnp.minimum(z, 7 - z)
    d = (i + 1) // 2
    both = z + d * (1 - 2 * (i % 2))
    return jnp.where(i <= 2 * near, both, jnp.where(z <= 3, i, 7 - i))


def gather_kernel(
    counts_ref, q_ref, k_ref, v_ref, sp_ref, mp_ref, w_ref,
    kv_ref, qs_ref, list_ref, w2_ref,
    mine, list_v,
    z_send, z_recv, zf_send, xr_send, xl_send, xl_recv, xr_recv,
    fk_send, fk_recv, fv_send, fv_recv, c_send, c_recv,
    q_send, q_recv, w_send, w_recv, wc_send, wc_recv, local_sem,
):
    s = lax.axis_index("seq")
    p = lax.axis_index("pass")
    h = lax.axis_index("head")
    x, z = s // NZ, s % NZ
    zh, y = h // NY, h % NY
    g = head_of_row(z)
    a, b = first_row(g), last_row(g)
    right = ((x + 1) % NX) * NZ + z
    left = ((x + 3) % NX) * NZ + z

    def dev(seq=s, core=p, head=h):
        return {"seq": seq, "pass": core, "head": head}

    barrier = pltpu.get_barrier_semaphore()
    for d in range(1, NZ):
        pl.semaphore_signal(barrier, inc=1, device_id=dev(seq=x * NZ + (z + d) % NZ), device_id_type=MESH)
    for d in range(1, NY):
        pl.semaphore_signal(barrier, inc=1, device_id=dev(head=zh * NY + (y + d) % NY), device_id_type=MESH)
    for seq in (right, left):
        pl.semaphore_signal(barrier, inc=1, device_id=dev(seq=seq), device_id_type=MESH)
    pl.semaphore_signal(barrier, inc=1, device_id=dev(core=1 - p), device_id_type=MESH)

    for n in range(3):
        cols = slice(n * HD, (n + 1) * HD)
        mine[n, :TILE, :] = k_ref[:, cols]
        mine[n, TILE:, :] = v_ref[:, cols].T

    pl.semaphore_wait(barrier, NZ - 1 + NY - 1 + 3)

    def remote(src, dst, send, recv, target):
        return pltpu.make_async_remote_copy(
            src_ref=src, dst_ref=dst, send_sem=send, recv_sem=recv, device_id=target, device_id_type=MESH
        )

    def entry_copy(n):
        e = jnp.maximum(first_row(n), jnp.minimum(z, last_row(n)))
        return e, remote(mine.at[n], kv_ref.at[s], z_send.at[n], z_recv.at[z], dev(seq=x * NZ + e))

    def up_copy(row_from, src, send):
        return remote(src, kv_ref.at[x * NZ + row_from], send, z_recv.at[row_from], dev(seq=s + 1))

    def down_copy(row_from, src, send):
        return remote(src, kv_ref.at[x * NZ + row_from], send, z_recv.at[row_from], dev(seq=s - 1))

    own_copy = pltpu.make_async_copy(mine.at[g], kv_ref.at[s], local_sem.at[0])
    own_copy.start()

    @pl.when(z < b)
    def _():
        up_copy(z, mine.at[g], z_send.at[3]).start()

    @pl.when(z > a)
    def _():
        down_copy(z, mine.at[g], z_send.at[4]).start()

    for n in range(3):
        e, copy = entry_copy(n)

        @pl.when(e != z)
        def _():
            copy.start()

    def query_copies(n):
        row, slot = query_place(z, n)
        src = q_ref.at[:, n * HD:(n + 1) * HD]
        away = remote(src, qs_ref.at[slot], q_send.at[n], q_recv.at[slot], dev(seq=x * NZ + row))
        here = pltpu.make_async_copy(src, qs_ref.at[slot], q_send.at[n])
        return row, away, here

    for n in range(3):
        row, away, here = query_copies(n)

        @pl.when(row != z)
        def _():
            away.start()

        @pl.when(row == z)
        def _():
            here.start()

    half_rows = 3 * HD // 2
    rows_mine = pl.ds(pl.multiple_of(p * half_rows, half_rows), half_rows)
    rows_other = pl.ds(pl.multiple_of((1 - p) * half_rows, half_rows), half_rows)

    def w_cols(yy, part):
        zz = zh if part == 0 else 1 - zh
        return pl.ds(pl.multiple_of((zz * NY + yy) * (3 * HD), 3 * HD), 3 * HD)

    def part_cols(part):
        return slice(part * 3 * HD, (part + 1) * 3 * HD)

    def w_copy(d, part):
        yy = (y + d) % NY
        return remote(
            w_ref.at[rows_mine, w_cols(yy, part)], w2_ref.at[y, rows_mine, part_cols(part)],
            w_send.at[2 * d + part], w_recv.at[2 * d + part], dev(head=zh * NY + yy),
        )

    def w_arrival(d, part):
        yy = (y + NY - d) % NY
        return remote(
            w_ref.at[rows_mine, w_cols(yy, part)], w2_ref.at[yy, rows_mine, part_cols(part)],
            w_send.at[2 * d + part], w_recv.at[2 * d + part], dev(head=zh * NY + yy),
        )

    def w_swap(d, rows):
        yy = (y + NY - d) % NY
        return remote(
            w2_ref.at[yy, rows], w2_ref.at[yy, rows], wc_send.at[d], wc_recv.at[d], dev(core=1 - p)
        )

    def w_local(part):
        return pltpu.make_async_copy(
            w_ref.at[:, w_cols(y, part)], w2_ref.at[y, :, part_cols(part)], local_sem.at[1 + part]
        )

    for part in range(2):
        w_local(part).start()
        for d in range(1, NY):
            w_copy(d, part).start()

    lane = lax.broadcasted_iota(I32, (1, 128), 1)
    tiles = jnp.full((1, 128), -1, I32)
    for j in range(SLOTS):
        row = slot_row(z, g, j)
        tile = jnp.where((row >= 0) & (row < NZ), x * NZ + row, -1)
        tiles = jnp.where(lane == j, tile, tiles)

    def hits(pairs, live_count, shift):
        live = lax.broadcasted_iota(I32, (pairs.shape[0], 1), 0) < live_count
        row_hits = ((pairs[:, 0:1] == tiles) & live).astype(F32)
        col_hits = (pairs[:, 1:2] + shift == lane).astype(F32)
        return lax.dot_general(row_hits, col_hits, (((0,), (0,)), ((), ())), preferred_element_type=F32)[:8]

    is_edit = (p == 1).astype(F32)
    total = hits(sp_ref[p], counts_ref[p], 0) + is_edit * hits(mp_ref[...], counts_ref[2], NT)
    allowed = (total > 0.5).astype(F32)
    earlier = lax.broadcasted_iota(I32, (128, 128), 0) < lax.broadcasted_iota(I32, (128, 128), 1)
    rank = jnp.dot(allowed, earlier.astype(F32), preferred_element_type=F32)
    lanes = lax.broadcasted_iota(I32, (8, 128), 1)
    lanes_f = lanes.astype(F32)
    picked = allowed * lanes_f
    listing = jnp.where(lanes == 127, jnp.sum(allowed, axis=1, keepdims=True), 0.0)

    def put(at, listing):
        found = jnp.sum(jnp.where(rank == at.astype(F32), picked, 0.0), axis=1, keepdims=True)
        return jnp.where(lanes == at, found, listing)

    listing = lax.fori_loop(0, ENTRIES, put, listing)
    list_v[...] = listing.astype(I32)
    list_copy = pltpu.make_async_copy(list_v, list_ref, local_sem.at[3])
    list_copy.start()

    def chip_copy(tile):
        return remote(kv_ref.at[tile], kv_ref.at[NT + tile], c_send.at[tile], c_recv.at[tile], dev(core=1 - p))

    def chip_start(tile):
        @pl.when(p == 0)
        def _():
            chip_copy(tile).start()

    def tile_at(dx, r):
        return ((x + dx) % NX) * NZ + r

    def right_copy(tile, r):
        return remote(kv_ref.at[tile], kv_ref.at[tile], xr_send.at[r], xl_recv.at[r], dev(seq=right))

    def left_copy(tile, r):
        return remote(kv_ref.at[tile], kv_ref.at[tile], xl_send.at[r], xr_recv.at[r], dev(seq=left))

    def key_copy(tile, r):
        part = kv_ref.at[tile, :TILE]
        return remote(part, part, fk_send.at[r], fk_recv.at[r], dev(seq=right))

    def value_copy(tile, r):
        part = kv_ref.at[tile, TILE:]
        return remote(part, part, fv_send.at[r], fv_recv.at[r], dev(seq=left))

    def step(i, carry):
        @pl.when(i < NZ)
        def _():
            r = row_order(i, z)
            tile = x * NZ + r

            @pl.when(r == z)
            def _():
                own_copy.wait()

            @pl.when(r != z)
            def _():
                remote(kv_ref.at[tile], kv_ref.at[tile], z_send.at[0], z_recv.at[r], dev(seq=s)).wait_recv()

            @pl.when((r < z) & (z < b))
            def _():
                up_copy(r, kv_ref.at[tile], zf_send.at[r]).start()

            @pl.when((r > z) & (z > a))
            def _():
                down_copy(r, kv_ref.at[tile], zf_send.at[r]).start()

            right_copy(tile, r).start()
            left_copy(tile, r).start()
            chip_start(tile)

        @pl.when((i >= 1) & (i <= NZ))
        def _():
            r = row_order(i - 1, z)
            from_left, from_right = tile_at(3, r), tile_at(1, r)
            right_copy(from_left, r).wait_recv()
            key_copy(from_left, r).start()
            chip_start(from_left)
            left_copy(from_right, r).wait_recv()
            value_copy(from_right, r).start()
            chip_start(from_right)

        @pl.when(i >= 2)
        def _():
            r = row_order(i - 2, z)
            far = tile_at(2, r)
            key_copy(far, r).wait_recv()
            value_copy(far, r).wait_recv()
            chip_start(far)

        return carry

    lax.fori_loop(0, NZ + 2, step, 0)

    for d in range(1, NY):
        for part in range(2):
            w_arrival(d, part).wait_recv()
        w_swap(d, rows_mine).start()

    def drain(r, carry):
        tile = x * NZ + r

        @pl.when((r < z) & (z < b))
        def _():
            up_copy(r, kv_ref.at[tile], zf_send.at[r]).wait_send()

        @pl.when((r > z) & (z > a))
        def _():
            down_copy(r, kv_ref.at[tile], zf_send.at[r]).wait_send()

        right_copy(tile, r).wait_send()
        left_copy(tile, r).wait_send()
        key_copy(tile_at(3, r), r).wait_send()
        value_copy(tile_at(1, r), r).wait_send()
        return carry

    lax.fori_loop(0, NZ, drain, 0)

    def drain_chip(t, carry):
        @pl.when(p == 0)
        def _():
            chip_copy(t).wait_send()

        @pl.when(p == 1)
        def _():
            chip_copy(t).wait_recv()

        return carry

    lax.fori_loop(0, NT, drain_chip, 0)

    @pl.when(z < b)
    def _():
        up_copy(z, mine.at[g], z_send.at[3]).wait_send()

    @pl.when(z > a)
    def _():
        down_copy(z, mine.at[g], z_send.at[4]).wait_send()

    for n in range(3):
        e, copy = entry_copy(n)

        @pl.when(e != z)
        def _():
            copy.wait_send()

        row, away, here = query_copies(n)

        @pl.when(row != z)
        def _():
            away.wait_send()

        @pl.when(row == z)
        def _():
            here.wait()

    for j in range(SLOTS):
        row = slot_row(z, g, j)

        @pl.when((row >= 0) & (row < NZ) & (row != z))
        def _():
            remote(
                q_ref.at[:, :HD], qs_ref.at[j], q_send.at[0], q_recv.at[j], dev(seq=s)
            ).wait_recv()

    list_copy.wait()
    for part in range(2):
        w_local(part).wait()
    for d in range(1, NY):
        for part in range(2):
            w_copy(d, part).wait_send()
        w_swap(d, rows_mine).wait_send()
        w_swap(d, rows_other).wait_recv()


def attention_kernel(list_ref, q_ref, kv_ref, o_ref, scores):
    def slot(j, carry):
        n = list_ref[j, 127]

        @pl.when(n > 0)
        def _():
            query = q_ref[j].T

            def score(i, top):
                t = list_ref[j, i]
                got = jnp.dot(kv_ref[t, :TILE, :], query, preferred_element_type=F32)
                scores[i] = got
                return jnp.maximum(top, jnp.max(got.reshape(16, 8, TILE), axis=0))

            top = lax.fori_loop(0, n, score, jnp.full((8, TILE), -3e38, F32))
            shift = jnp.max(top, axis=0, keepdims=True) * EXP2_SCALE

            def gather(i, state):
                total, acc = state
                t = list_ref[j, i]
                exps = jnp.exp2(scores[i] * EXP2_SCALE - shift)
                total = total + jnp.sum(exps.reshape(16, 8, TILE), axis=0)
                acc = acc + jnp.dot(kv_ref[t, TILE:, :], exps.astype(BF16), preferred_element_type=F32)
                return total, acc

            total, acc = lax.fori_loop(
                0, n, gather, (jnp.zeros((8, TILE), F32), jnp.zeros((HD, TILE), F32))
            )
            row_total = jnp.sum(total, axis=0, keepdims=True)
            o_ref[j] = (acc / row_total).T.astype(BF16)

        return carry

    lax.fori_loop(0, SLOTS, slot, 0)


def project_kernel(
    o_ref, w2_ref, out_ref,
    w_v, full, give, got,
    o_send, o_recv, y_send, y_recv, h_send, h_recv, local_sem,
):
    s = lax.axis_index("seq")
    p = lax.axis_index("pass")
    h = lax.axis_index("head")
    x, z = s // NZ, s % NZ
    zh, y = h // NY, h % NY
    g = head_of_row(z)
    partner = (1 - zh) * NY + y

    def dev(seq=s, head=h):
        return {"seq": seq, "pass": p, "head": head}

    w_copy = pltpu.make_async_copy(w2_ref, w_v, local_sem.at[0])
    w_copy.start()
    barrier = pltpu.get_barrier_semaphore()
    for d in range(1, NZ):
        pl.semaphore_signal(barrier, inc=1, device_id=dev(seq=x * NZ + (z + d) % NZ), device_id_type=MESH)
    for d in range(1, NY):
        pl.semaphore_signal(barrier, inc=1, device_id=dev(head=zh * NY + (y + d) % NY), device_id_type=MESH)
    pl.semaphore_signal(barrier, inc=1, device_id=dev(head=partner), device_id_type=MESH)
    pl.semaphore_wait(barrier, NZ - 1 + NY)

    def remote(src, dst, send, recv, target):
        return pltpu.make_async_remote_copy(
            src_ref=src, dst_ref=dst, send_sem=send, recv_sem=recv, device_id=target, device_id_type=MESH
        )

    def back(j):
        row = slot_row(z, g, j)
        live = (row >= 0) & (row < NZ)
        dst = full.at[3 * y + g]
        away = remote(o_ref.at[j], dst, o_send.at[j], o_recv.at[g], dev(seq=x * NZ + row))
        here = pltpu.make_async_copy(o_ref.at[j], dst, o_send.at[j])
        return row, live, away, here

    for j in range(SLOTS):
        row, live, away, here = back(j)

        @pl.when(live & (row != z))
        def _():
            away.start()

        @pl.when(live & (row == z))
        def _():
            here.start()

    def y_copy(n, d):
        block = full.at[3 * y + n]
        return remote(
            block, block, y_send.at[3 * n + d - 1], y_recv.at[3 * n + d - 1],
            dev(head=zh * NY + (y + d) % NY),
        )

    def y_arrival(n, d):
        block = full.at[3 * ((y + NY - d) % NY) + n]
        return remote(
            block, block, y_send.at[3 * n + d - 1], y_recv.at[3 * n + d - 1],
            dev(head=zh * NY + (y + d) % NY),
        )

    for j in range(SLOTS):
        row, live, away, here = back(j)

        @pl.when(live & (row == z))
        def _():
            here.wait()

    for n in range(3):
        row, _slot = query_place(z, n)
        block = full.at[3 * y + n]

        @pl.when(row != z)
        def _():
            remote(block, block, o_send.at[0], o_recv.at[n], dev(seq=s)).wait_recv()

        for d in range(1, NY):
            y_copy(n, d).start()

    w_copy.wait()
    for n in range(3):
        for d in range(1, NY):
            y_arrival(n, d).wait_recv()

    def projected(part):
        acc = jnp.zeros((TILE, 3 * HD), F32)
        for n in range(3 * NY):
            acc = acc + jnp.dot(
                full[n], w_v[n * HD:(n + 1) * HD, part * 3 * HD:(part + 1) * 3 * HD],
                preferred_element_type=F32,
            )
        return acc

    give[...] = projected(1).astype(BF16)
    swap = remote(give, got, h_send, h_recv, dev(head=partner))
    swap.start()
    own = projected(0)
    swap.wait_recv()
    out_ref[...] = (own + got[...].astype(F32)).astype(BF16)

    swap.wait_send()
    for j in range(SLOTS):
        row, live, away, here = back(j)

        @pl.when(live & (row != z))
        def _():
            away.wait_send()

    for n in range(3):
        for d in range(1, NY):
            y_copy(n, d).wait_send()


def on_device(queries, keys, values, self_pairs, mask_pairs, counts, out_weight):
    vmem = pl.BlockSpec(memory_space=pltpu.VMEM)
    smem = pl.BlockSpec(memory_space=pltpu.SMEM)
    hbm = pl.BlockSpec(memory_space=pl.ANY)
    dma = pltpu.SemaphoreType.DMA
    shape = jax.ShapeDtypeStruct
    big = 48 * 1024 * 1024

    tiles, slots, listing, weights = pl.pallas_call(
        gather_kernel,
        out_shape=(
            shape((ENTRIES, 2 * TILE, HD), BF16),
            shape((SLOTS, TILE, HD), BF16),
            shape((8, 128), I32),
            shape((NY, 3 * HD, 6 * HD), BF16),
        ),
        in_specs=[smem, vmem, vmem, vmem, vmem, vmem, hbm],
        out_specs=(hbm, hbm, hbm, hbm),
        scratch_shapes=[
            pltpu.VMEM((3, 2 * TILE, HD), BF16),
            pltpu.VMEM((8, 128), I32),
            dma((5,)), dma((NZ,)), dma((NZ,)),
            dma((NZ,)), dma((NZ,)), dma((NZ,)), dma((NZ,)),
            dma((NZ,)), dma((NZ,)), dma((NZ,)), dma((NZ,)),
            dma((NT,)), dma((NT,)),
            dma((3,)), dma((SLOTS,)),
            dma((2 * NY,)), dma((2 * NY,)), dma((NY,)), dma((NY,)), dma((4,)),
        ],
        compiler_params=pltpu.CompilerParams(collective_id=0, has_side_effects=True),
        name="gather_tiles",
    )(counts, queries[0], keys[0], values[0], self_pairs, mask_pairs, out_weight)

    attended = pl.pallas_call(
        attention_kernel,
        out_shape=shape((SLOTS, TILE, HD), BF16),
        in_specs=[smem, vmem, vmem],
        out_specs=vmem,
        scratch_shapes=[pltpu.VMEM((ENTRIES, TILE, TILE), F32)],
        compiler_params=pltpu.CompilerParams(vmem_limit_bytes=big),
        name="attention",
    )(listing, slots, tiles)

    projected = pl.pallas_call(
        project_kernel,
        out_shape=shape((TILE, 3 * HD), BF16),
        in_specs=[vmem, hbm],
        out_specs=vmem,
        scratch_shapes=[
            pltpu.VMEM((3 * NY * HD, 6 * HD), BF16),
            pltpu.VMEM((3 * NY, TILE, HD), BF16),
            pltpu.VMEM((TILE, 3 * HD), BF16),
            pltpu.VMEM((TILE, 3 * HD), BF16),
            dma((SLOTS,)), dma((3,)), dma((9,)), dma((9,)), dma, dma, dma((1,)),
        ],
        compiler_params=pltpu.CompilerParams(collective_id=1, has_side_effects=True, vmem_limit_bytes=big),
        name="project",
    )(attended, weights.reshape(3 * NY * HD, 6 * HD))
    return projected[None]


def solution(mesh):
    in_specs = (
        P("pass", "seq", "head"),
        P("pass", "seq", "head"),
        P("pass", "seq", "head"),
        P(),
        P(),
        P(),
        P("head", None),
    )
    out_specs = P("pass", "seq", "head")
    return jax.shard_map(
        on_device, mesh=mesh, in_specs=in_specs, out_specs=out_specs, check_vma=False
    )
```

time: 1100 us -> 104 us (0.09)
  the two profiles are of different devices: /device:TPU:4 before, /device:TPU:65 now
where the time goes in v1:
time: 104 us
  Pallas kernels  96.5 us (93%)
  local copies, waits for them, and re-layouts  7.31 us (7%)
    pallas_call x1, Pallas kernels, on_device(): pl.pallas_call(gather_kernel, out_shape=(shape((ENTRIES, 2 * TILE, HD), B...  47.8 us
    pallas_call x1, Pallas kernels, on_device(): pl.pallas_call(project_kernel, out_shape=shape((TILE, 3 * HD), BF16), in_...  39.5 us
    pallas_call x1, Pallas kernels, on_device(): pl.pallas_call(attention_kernel, out_shape=shape((SLOTS, TILE, HD), BF16)...  9.19 us
    unnamed x11, local copies, waits for them, and re-layouts  7.31 us

profile of v1, /device:TPU:65, one launch (start us, length us, event | category | flops | bytes accessed | tf_op | source)
XLA Modules:
  0.0 103.9 jit_solution(9730374128205859813)
XLA Ops:
  0.0 1.4 %copy.9.mp_ref = s32[128,2]{1,0:T(8,128)} copy(s32[128,2]{0,1:T(2,128)} %param.11) | data formatting | bytes 2048 | tf_op args[4]
  1.4 1.5 %copy.8.sp_ref = s32[2,160,2]{2,1,0:T(8,128)} copy(s32[2,160,2]{1,2,0:T(2,128)} %param.10) | data formatting | bytes 5120 | tf_op args[3]
  2.9 47.8 %gather_tiles.1 = (bf16[64,256,128]{2,1,0:T(8,128)(2,1)}, bf16[4,128,128]{2,1,0:T(8,128)(2,1)}, s32[8,128]{1,0:T(8,128)}, bf16[4,384,768]{2,1,0:T(8,128)(2,1)}) custom-call(s32[3]{0:T(128)} %counts_ref.1, bf16[128,384]{1,0:T(8,128)(2,1)} %bitcast.7, bf16[128,384]{1,0:T(8,128)(2,1)} %bitcast.8, bf16[128,384]{1,0:T(8,128)(2,1)} %bitcast.9, ...), custom_call_target="tpu_custom_call" | custom-call | tf_op jit(solution)/shard_map/gather_tiles/pallas_call | solution.py:537
  50.7 0.0 copy-start
  50.8 2.2 %copy-done = bf16[64,256,128]{2,1,0:T(8,128)(2,1)S(1)} copy-done((bf16[64,256,128]{2,1,0:T(8,128)(2,1)S(1)}, bf16[64,256,128]{2,1,0:T(8,128)(2,1)}, u32[]{:S(2)}) %copy-start) | copy-done | bytes 4194328
  52.9 0.0 copy-start.2
  52.9 0.9 copy-done.2
  53.8 0.0 copy-start.3
  53.8 0.7 copy-done.3
  54.5 0.0 copy-start.1
  54.5 9.2 %attention.1.o_ref = bf16[4,128,128]{2,1,0:T(8,128)(2,1)S(1)} custom-call(s32[8,128]{1,0:T(8,128)S(1)} %copy-done.3, bf16[4,128,128]{2,1,0:T(8,128)(2,1)S(1)} %copy-done.2, bf16[64,256,128]{2,1,0:T(8,128)(2,1)S(1)} %copy-done), custom_call_target="tpu_custom_call" | custom-call | tf_op jit(solution)/shard_map/attention/pallas_call | solution.py:561
  63.7 0.0 copy-done.1
  63.7 39.5 %project.1 = bf16[128,384]{1,0:T(8,128)(2,1)S(1)} custom-call(bf16[4,128,128]{2,1,0:T(8,128)(2,1)S(1)} %attention.1.o_ref, bf16[1536,768]{1,0:T(8,128)(2,1)S(1)} %bitcast.5), custom_call_target="tpu_custom_call" | custom-call | tf_op jit(solution)/shard_map/project/pallas_call | solution.py:571
  103.2 0.6 copy.11
Async XLA Ops:
  50.7 2.2 %copy-start = (bf16[64,256,128]{2,1,0:T(8,128)(2,1)S(1)}, bf16[64,256,128]{2,1,0:T(8,128)(2,1)}, u32[]{:S(2)}) copy-start(bf16[64,256,128]{2,1,0:T(8,128)(2,1)} %get-tuple-element.11.kv_ref) | copy-start | bytes 12582916
  52.9 0.9 copy-start.2
  53.8 0.7 copy-start.3
  54.5 9.2 %copy-start.1 = (bf16[4,384,768]{2,1,0:T(8,128)(2,1)S(1)}, bf16[4,384,768]{2,1,0:T(8,128)(2,1)}, u32[]{:S(2)}) copy-start(bf16[4,384,768]{2,1,0:T(8,128)(2,1)} %get-tuple-element.12) | copy-start | bytes 7077892

commit v2 on v1

v2 whole, which is shorter than its diff:
```python
import functools
import math

import jax
import jax.numpy as jnp
from jax import lax
from jax.experimental import pallas as pl
from jax.experimental.pallas import tpu as pltpu
from jax.sharding import PartitionSpec as P

HD = 128
TILE = 128
NX = 4
NZ = 8
NY = 4
SLOTS = 4
ENTRIES = 2 * NZ
BF16 = jnp.bfloat16
F32 = jnp.float32
I32 = jnp.int32
EXP2_SCALE = HD ** -0.5 * math.log2(math.e)
NOTHING = -1e30
MESH = pl.DeviceIdType.MESH


def head_of_row(z):
    return (3 * z + 1) // 8


def first_row(g):
    return (8 * g + 1) // 3


def last_row(g):
    return (8 * g + 9) // 3 - 1


def query_place(zq, g):
    if g == 0:
        return zq // 3, zq % 3
    if g == 1:
        return 3 + zq // 4, zq % 4
    return 7 - (7 - zq) // 3, (7 - zq) % 3


def slot_row(z, g, j):
    low = 3 * z + j
    mid = 4 * (z - 3) + j
    high = 7 - (3 * (7 - z) + j)
    row = jnp.where(g == 0, low, jnp.where(g == 1, mid, high))
    return jnp.where((j == 3) & (g != 1), -1, row)


def row_order(i, z):
    near = jnp.minimum(z, 7 - z)
    d = (i + 1) // 2
    both = z + d * (1 - 2 * (i % 2))
    return jnp.where(i <= 2 * near, both, jnp.where(z <= 3, i, 7 - i))


def remote(src, dst, send, recv, target):
    return pltpu.make_async_remote_copy(
        src_ref=src, dst_ref=dst, send_sem=send, recv_sem=recv, device_id=target, device_id_type=MESH
    )


def greet(devices):
    barrier = pltpu.get_barrier_semaphore()
    for device in devices:
        pl.semaphore_signal(barrier, inc=1, device_id=device, device_id_type=MESH)
    return lambda: pl.semaphore_wait(barrier, len(devices))


def gather_kernel(
    counts_ref, q_ref, k_ref, v_ref, sp_ref, mp_ref, w_ref,
    kv_ref, qs_ref, list_ref, w2_ref,
    mine, list_v,
    z_send, z_recv, zf_send, c_send, c_recv,
    q_send, q_recv, qx_send, qx_recv, w_send, w_recv, wc_send, wc_recv, local_sem,
):
    s = lax.axis_index("seq")
    p = lax.axis_index("pass")
    h = lax.axis_index("head")
    x, z = s // NZ, s % NZ
    zh, y = h // NY, h % NY
    g = head_of_row(z)
    a, b = first_row(g), last_row(g)

    def dev(seq=s, core=p, head=h):
        return {"seq": seq, "pass": core, "head": head}

    def along_x(d):
        return dev(seq=((x + d) % NX) * NZ + z)

    def along_y(d):
        return dev(head=zh * NY + (y + d) % NY)

    met = greet(
        [dev(seq=x * NZ + (z + d) % NZ) for d in range(1, NZ)]
        + [along_x(d) for d in range(1, NX)]
        + [along_y(d) for d in range(1, NY)]
        + [dev(core=1 - p)]
    )

    for n in range(3):
        cols = slice(n * HD, (n + 1) * HD)
        mine[n, :TILE, :] = k_ref[:, cols]
        mine[n, TILE:, :] = v_ref[:, cols].T
    own_copy = pltpu.make_async_copy(mine.at[g], kv_ref.at[z], local_sem.at[0])
    own_copy.start()

    met()

    def query_copies(n):
        row, slot = query_place(z, n)
        src, dst = q_ref.at[:, n * HD:(n + 1) * HD], qs_ref.at[x * SLOTS + slot]
        away = remote(src, dst, q_send.at[n], q_recv.at[slot], dev(seq=x * NZ + row))
        here = pltpu.make_async_copy(src, dst, q_send.at[n])
        return row, away, here

    for n in range(3):
        row, away, here = query_copies(n)
        pl.when(row != z)(away.start)
        pl.when(row == z)(here.start)

    def up_copy(r, src, send):
        return remote(src, kv_ref.at[r], send, z_recv.at[r], dev(seq=s + 1))

    def down_copy(r, src, send):
        return remote(src, kv_ref.at[r], send, z_recv.at[r], dev(seq=s - 1))

    def entry_copy(n):
        e = jnp.maximum(first_row(n), jnp.minimum(z, last_row(n)))
        return e, remote(mine.at[n], kv_ref.at[z], z_send.at[n], z_recv.at[z], dev(seq=x * NZ + e))

    pl.when(z < b)(up_copy(z, mine.at[g], z_send.at[3]).start)
    pl.when(z > a)(down_copy(z, mine.at[g], z_send.at[4]).start)
    for n in range(3):
        e, copy = entry_copy(n)
        pl.when(e != z)(copy.start)

    half_rows = 3 * HD // 2
    rows_mine = pl.ds(pl.multiple_of(p * half_rows, half_rows), half_rows)
    rows_other = pl.ds(pl.multiple_of((1 - p) * half_rows, half_rows), half_rows)

    def w_cols(yy, part):
        zz = zh if part == 0 else 1 - zh
        return pl.ds(pl.multiple_of((zz * NY + yy) * (3 * HD), 3 * HD), 3 * HD)

    def part_cols(part):
        return slice(part * 3 * HD, (part + 1) * 3 * HD)

    def w_copy(d, part):
        return remote(
            w_ref.at[rows_mine, w_cols((y + d) % NY, part)], w2_ref.at[y, rows_mine, part_cols(part)],
            w_send.at[2 * d + part], w_recv.at[2 * d + part], along_y(d),
        )

    def w_arrival(d, part):
        place = w2_ref.at[(y + NY - d) % NY, rows_mine, part_cols(part)]
        return remote(place, place, w_send.at[2 * d + part], w_recv.at[2 * d + part], along_y(d))

    def w_swap(d, rows):
        place = w2_ref.at[(y + NY - d) % NY, rows]
        return remote(place, place, wc_send.at[d], wc_recv.at[d], dev(core=1 - p))

    def w_local(part):
        return pltpu.make_async_copy(
            w_ref.at[:, w_cols(y, part)], w2_ref.at[y, :, part_cols(part)], local_sem.at[1 + part]
        )

    for part in range(2):
        for d in range(1, NY):
            w_copy(d, part).start()
        w_local(part).start()

    slots = lax.broadcasted_iota(I32, (NX * SLOTS, 1), 0)
    tiles = jnp.full((NX * SLOTS, 1), -1, I32)
    for j in range(SLOTS):
        row = slot_row(z, g, j)
        live = (row >= 0) & (row < NZ)
        tiles = jnp.where(((slots & 3) == j) & live, (slots >> 2) * NZ + row, tiles)

    def hits(queries, keys, live_count, shift):
        live = lax.broadcasted_iota(I32, queries.shape, 1) < live_count
        row_hits = ((queries == tiles) & live).astype(F32)
        row = keys - x * NZ
        row = jnp.where((row >= 0) & (row < NZ), row + shift, -1)
        col_hits = (lax.broadcasted_iota(I32, (128, 1), 0) == row).astype(F32)
        return lax.dot_general(row_hits, col_hits, (((1,), (1,)), ((), ())), preferred_element_type=F32)

    is_edit = (p == 1).astype(F32)
    total = hits(sp_ref[p, 0:1], sp_ref[p, 1:2], counts_ref[p], 0)
    total = total + is_edit * hits(mp_ref[0:1], mp_ref[1:2], counts_ref[2], NZ)
    allowed = (total > 0.5).astype(F32)
    earlier = lax.broadcasted_iota(I32, (128, 128), 0) < lax.broadcasted_iota(I32, (128, 128), 1)
    rank = jnp.dot(allowed, earlier.astype(F32), preferred_element_type=F32)
    lanes = lax.broadcasted_iota(I32, (NX * SLOTS, 128), 1)
    picked = allowed * lanes.astype(F32)
    listing = jnp.where(lanes == 127, jnp.sum(allowed, axis=1, keepdims=True), 0.0)
    for at in range(ENTRIES):
        found = jnp.sum(jnp.where(rank == at, picked, 0.0), axis=1, keepdims=True)
        listing = jnp.where(lanes == at, found, listing)
    list_v[...] = listing.astype(I32)
    list_copy = pltpu.make_async_copy(list_v, list_ref, local_sem.at[3])
    list_copy.start()

    def chip_copy(r):
        return remote(kv_ref.at[r], kv_ref.at[NZ + r], c_send.at[r], c_recv.at[r], dev(core=1 - p))

    own_copy.wait()
    pl.when(p == 0)(chip_copy(z).start)

    def pass_on(i, carry):
        r = row_order(i, z)
        place = kv_ref.at[r]
        remote(place, place, z_send.at[0], z_recv.at[r], dev()).wait_recv()
        pl.when((r < z) & (z < b))(up_copy(r, place, zf_send.at[r]).start)
        pl.when((r > z) & (z > a))(down_copy(r, place, zf_send.at[r]).start)
        pl.when(p == 0)(chip_copy(r).start)
        return carry

    lax.fori_loop(1, 3, pass_on, 0)

    def qx_copy(j, d):
        place = qs_ref.at[x * SLOTS + j]
        return remote(place, place, qx_send.at[3 * j + d - 1], qx_recv.at[3 * j + d - 1], along_x(d))

    def qx_arrival(j, d):
        place = qs_ref.at[((x + NX - d) % NX) * SLOTS + j]
        return remote(place, place, qx_send.at[3 * j + d - 1], qx_recv.at[3 * j + d - 1], along_x(d))

    def live_slot(j):
        row = slot_row(z, g, j)
        return row, (row >= 0) & (row < NZ)

    for n in range(3):
        row, away, here = query_copies(n)
        pl.when(row == z)(here.wait)

    for j in range(SLOTS):
        row, live = live_slot(j)
        place = qs_ref.at[x * SLOTS + j]

        @pl.when(live)
        def _():
            pl.when(row != z)(remote(place, place, q_send.at[0], q_recv.at[j], dev()).wait_recv)
            for d in range(1, NX):
                qx_copy(j, d).start()

    lax.fori_loop(3, NZ, pass_on, 0)

    for d in range(1, NY):
        for part in range(2):
            w_arrival(d, part).wait_recv()
        w_swap(d, rows_mine).start()

    def drain(r, carry):
        place = kv_ref.at[r]
        pl.when((r < z) & (z < b))(up_copy(r, place, zf_send.at[r]).wait_send)
        pl.when((r > z) & (z > a))(down_copy(r, place, zf_send.at[r]).wait_send)
        pl.when(p == 0)(chip_copy(r).wait_send)
        pl.when(p == 1)(chip_copy(r).wait_recv)
        return carry

    lax.fori_loop(0, NZ, drain, 0)
    pl.when(z < b)(up_copy(z, mine.at[g], z_send.at[3]).wait_send)
    pl.when(z > a)(down_copy(z, mine.at[g], z_send.at[4]).wait_send)
    for n in range(3):
        e, copy = entry_copy(n)
        pl.when(e != z)(copy.wait_send)
        row, away, here = query_copies(n)
        pl.when(row != z)(away.wait_send)

    for j in range(SLOTS):
        row, live = live_slot(j)

        @pl.when(live)
        def _():
            for d in range(1, NX):
                qx_copy(j, d).wait_send()
                qx_arrival(j, d).wait_recv()

    list_copy.wait()
    for part in range(2):
        w_local(part).wait()
    for d in range(1, NY):
        for part in range(2):
            w_copy(d, part).wait_send()
        w_swap(d, rows_mine).wait_send()
        w_swap(d, rows_other).wait_recv()


def attention_kernel(list_ref, q_ref, kv_ref, o_ref, stat_ref):
    stat_ref[...] = jnp.full(stat_ref.shape, NOTHING, F32)

    def slot(j, carry):
        n = list_ref[j, 127]

        @pl.when(n == 0)
        def _():
            o_ref[j] = jnp.zeros((HD, TILE), BF16)

        @pl.when(n > 0)
        def _():
            query = q_ref[j].T

            def two_tiles(i, state):
                top, total, acc = state
                t, u = list_ref[j, 2 * i], list_ref[j, 2 * i + 1]
                keys = jnp.concatenate([kv_ref[t, :TILE, :], kv_ref[u, :TILE, :]], axis=0)
                values = jnp.concatenate([kv_ref[t, TILE:, :], kv_ref[u, TILE:, :]], axis=1)
                scores = jnp.dot(keys, query, preferred_element_type=F32) * EXP2_SCALE
                second = jnp.where(2 * i + 1 < n, scores[TILE:], NOTHING)
                scores = jnp.concatenate([scores[:TILE], second], axis=0)
                new_top = jnp.maximum(top, jnp.max(scores, axis=0, keepdims=True))
                faded = jnp.exp2(top - new_top)
                exps = jnp.exp2(scores - new_top)
                total = total * faded + jnp.sum(exps.reshape(32, 8, TILE), axis=0)
                acc = acc * faded + jnp.dot(values, exps.astype(BF16), preferred_element_type=F32)
                return new_top, total, acc

            top, total, acc = lax.fori_loop(
                0, (n + 1) // 2, two_tiles,
                (jnp.full((1, TILE), NOTHING, F32), jnp.zeros((8, TILE), F32), jnp.zeros((HD, TILE), F32)),
            )
            row_total = jnp.sum(total, axis=0, keepdims=True)
            o_ref[j] = (acc / row_total).astype(BF16)
            stat_ref[j // SLOTS, pl.ds(j % SLOTS, 1), :] = top + jnp.log2(row_total)

        return carry

    lax.fori_loop(0, NX * SLOTS, slot, 0)


def project_kernel(
    o_ref, stat_ref, w2_ref, out_ref,
    w_v, parts, part_stats, merged, full, give, got,
    x_send, x_recv, s_send, s_recv, o_send, o_recv, y_send, y_recv, h_send, h_recv, local_sem,
):
    s = lax.axis_index("seq")
    p = lax.axis_index("pass")
    h = lax.axis_index("head")
    x, z = s // NZ, s % NZ
    zh, y = h // NY, h % NY
    g = head_of_row(z)

    def dev(seq=s, head=h):
        return {"seq": seq, "pass": p, "head": head}

    def along_x(d):
        return dev(seq=((x + d) % NX) * NZ + z)

    def along_y(d):
        return dev(head=zh * NY + (y + d) % NY)

    partner = dev(head=(1 - zh) * NY + y)
    met = greet(
        [dev(seq=x * NZ + (z + d) % NZ) for d in range(1, NZ)]
        + [along_x(d) for d in range(1, NX)]
        + [along_y(d) for d in range(1, NY)]
        + [partner]
    )
    w_copy = pltpu.make_async_copy(w2_ref, w_v, local_sem.at[0])
    w_copy.start()
    met()

    def live_slot(j):
        row = slot_row(z, g, j)
        return row, (row >= 0) & (row < NZ)

    def stat_copy(d):
        return remote(
            stat_ref.at[(x + d) % NX], part_stats.at[d - 1], s_send.at[d - 1], s_recv.at[d - 1], along_x(d)
        )

    def part_copy(j, d):
        at = 3 * j + d - 1
        return remote(
            o_ref.at[((x + d) % NX) * SLOTS + j], parts.at[at], x_send.at[at], x_recv.at[at], along_x(d)
        )

    for d in range(1, NX):
        stat_copy(d).start()
    for j in range(SLOTS):
        row, live = live_slot(j)

        @pl.when(live)
        def _():
            for d in range(1, NX):
                part_copy(j, d).start()

    def back(j):
        row, live = live_slot(j)
        dst = full.at[3 * y + g]
        away = remote(merged.at[j], dst, o_send.at[j], o_recv.at[g], dev(seq=x * NZ + row))
        here = pltpu.make_async_copy(merged.at[j], dst, o_send.at[j])
        return row, live, away, here

    for d in range(1, NX):
        stat_copy(d).wait_recv()
    for j in range(SLOTS):
        row, live, away, here = back(j)

        @pl.when(live)
        def _():
            stats = [stat_ref[x, j:j + 1, :]] + [part_stats[d, j:j + 1, :] for d in range(3)]
            top = functools.reduce(jnp.maximum, stats)
            shares = [jnp.exp2(stat - top) for stat in stats]
            whole = sum(shares)
            for d in range(1, NX):
                part_copy(j, d).wait_recv()
            blocks = [o_ref[x * SLOTS + j]] + [parts[3 * j + d] for d in range(3)]
            mixed = sum(block.astype(F32) * (share / whole) for block, share in zip(blocks, shares))
            merged[j] = mixed.T.astype(BF16)
            pl.when(row != z)(away.start)
            pl.when(row == z)(here.start)

    def y_copy(n, d):
        block = full.at[3 * y + n]
        return remote(block, block, y_send.at[3 * n + d - 1], y_recv.at[3 * n + d - 1], along_y(d))

    def y_arrival(n, d):
        block = full.at[3 * ((y + NY - d) % NY) + n]
        return remote(block, block, y_send.at[3 * n + d - 1], y_recv.at[3 * n + d - 1], along_y(d))

    for j in range(SLOTS):
        row, live, away, here = back(j)
        pl.when(live & (row == z))(here.wait)

    for n in range(3):
        row, _slot = query_place(z, n)
        block = full.at[3 * y + n]
        pl.when(row != z)(remote(block, block, o_send.at[0], o_recv.at[n], dev()).wait_recv)
        for d in range(1, NY):
            y_copy(n, d).start()

    w_copy.wait()
    for n in range(3):
        for d in range(1, NY):
            y_arrival(n, d).wait_recv()

    def projected(part):
        acc = jnp.zeros((TILE, 3 * HD), F32)
        for n in range(3 * NY):
            acc = acc + jnp.dot(
                full[n], w_v[n * HD:(n + 1) * HD, part * 3 * HD:(part + 1) * 3 * HD],
                preferred_element_type=F32,
            )
        return acc

    give[...] = projected(1).astype(BF16)
    swap = remote(give, got, h_send, h_recv, partner)
    swap.start()
    own = projected(0)
    swap.wait_recv()
    out_ref[...] = (own + got[...].astype(F32)).astype(BF16)

    swap.wait_send()
    for d in range(1, NX):
        stat_copy(d).wait_send()
    for j in range(SLOTS):
        row, live, away, here = back(j)

        @pl.when(live)
        def _():
            for d in range(1, NX):
                part_copy(j, d).wait_send()
            pl.when(row != z)(away.wait_send)

    for n in range(3):
        for d in range(1, NY):
            y_copy(n, d).wait_send()


def on_device(queries, keys, values, self_pairs, mask_pairs, counts, out_weight):
    vmem = pl.BlockSpec(memory_space=pltpu.VMEM)
    smem = pl.BlockSpec(memory_space=pltpu.SMEM)
    hbm = pl.BlockSpec(memory_space=pl.ANY)
    dma = pltpu.SemaphoreType.DMA
    shape = jax.ShapeDtypeStruct
    big = 32 * 1024 * 1024

    tiles, slots, listing, weights = pl.pallas_call(
        gather_kernel,
        out_shape=(
            shape((ENTRIES, 2 * TILE, HD), BF16),
            shape((NX * SLOTS, TILE, HD), BF16),
            shape((NX * SLOTS, 128), I32),
            shape((NY, 3 * HD, 6 * HD), BF16),
        ),
        in_specs=[smem, vmem, vmem, vmem, vmem, vmem, hbm],
        out_specs=(hbm, hbm, hbm, hbm),
        scratch_shapes=[
            pltpu.VMEM((3, 2 * TILE, HD), BF16),
            pltpu.VMEM((NX * SLOTS, 128), I32),
            dma((5,)), dma((NZ,)), dma((NZ,)), dma((NZ,)), dma((NZ,)),
            dma((3,)), dma((SLOTS,)), dma((3 * SLOTS,)), dma((3 * SLOTS,)),
            dma((2 * NY,)), dma((2 * NY,)), dma((NY,)), dma((NY,)), dma((4,)),
        ],
        compiler_params=pltpu.CompilerParams(collective_id=0, has_side_effects=True),
        name="gather_tiles",
    )(
        counts, queries[0], keys[0], values[0],
        jnp.swapaxes(self_pairs, 1, 2), jnp.swapaxes(mask_pairs, 0, 1), out_weight,
    )

    attended, stats = pl.pallas_call(
        attention_kernel,
        out_shape=(shape((NX * SLOTS, HD, TILE), BF16), shape((NX, 8, TILE), F32)),
        in_specs=[smem, vmem, vmem],
        out_specs=(vmem, vmem),
        compiler_params=pltpu.CompilerParams(vmem_limit_bytes=big),
        name="attention",
    )(listing, slots, tiles)

    projected = pl.pallas_call(
        project_kernel,
        out_shape=shape((TILE, 3 * HD), BF16),
        in_specs=[vmem, vmem, hbm],
        out_specs=vmem,
        scratch_shapes=[
            pltpu.VMEM((3 * NY * HD, 6 * HD), BF16),
            pltpu.VMEM((3 * SLOTS, HD, TILE), BF16),
            pltpu.VMEM((3, 8, TILE), F32),
            pltpu.VMEM((SLOTS, TILE, HD), BF16),
            pltpu.VMEM((3 * NY, TILE, HD), BF16),
            pltpu.VMEM((TILE, 3 * HD), BF16),
            pltpu.VMEM((TILE, 3 * HD), BF16),
            dma((3 * SLOTS,)), dma((3 * SLOTS,)), dma((3,)), dma((3,)),
            dma((SLOTS,)), dma((3,)), dma((9,)), dma((9,)), dma, dma, dma((1,)),
        ],
        compiler_params=pltpu.CompilerParams(collective_id=1, has_side_effects=True, vmem_limit_bytes=big),
        name="project",
    )(attended, stats, weights.reshape(3 * NY * HD, 6 * HD))
    return projected[None]


def solution(mesh):
    in_specs = (
        P("pass", "seq", "head"),
        P("pass", "seq", "head"),
        P("pass", "seq", "head"),
        P(),
        P(),
        P(),
        P("head", None),
    )
    out_specs = P("pass", "seq", "head")
    return jax.shard_map(
        on_device, mesh=mesh, in_specs=in_specs, out_specs=out_specs, check_vma=False
    )
```

time: 104 us -> 85.7 us (0.82)
  the two profiles are of different devices: /device:TPU:65 before, /device:TPU:70 now
where the time goes in v2:
time: 85.7 us; the launch traced here: 85.4 us
  Pallas kernels  80.1 us (93%)
  local copies, waits for them, and re-layouts  5.26 us (6%)
    pallas_call x1, Pallas kernels, on_device(): pl.pallas_call(project_kernel, out_shape=shape((TILE, 3 * HD), BF16), in_...  46.2 us
    pallas_call x1, Pallas kernels, on_device(): pl.pallas_call(gather_kernel, out_shape=(shape((ENTRIES, 2 * TILE, HD), B...  30.2 us
    unnamed x9, local copies, waits for them, and re-layouts  5.26 us
    pallas_call x1, Pallas kernels, on_device(): pl.pallas_call(attention_kernel, out_shape=(shape((NX * SLOTS, HD, TILE),...  3.74 us

profile of v2, /device:TPU:70, one launch (start us, length us, event | category | flops | bytes accessed | tf_op | source)
XLA Modules:
  0.0 85.4 jit_solution(3978523910268492998)
XLA Ops:
  0.0 30.2 %gather_tiles.1 = (bf16[16,256,128]{2,1,0:T(8,128)(2,1)}, bf16[16,128,128]{2,1,0:T(8,128)(2,1)}, s32[16,128]{1,0:T(8,128)}, bf16[4,384,768]{2,1,0:T(8,128)(2,1)}) custom-call(s32[3]{0:T(128)} %counts_ref.1, bf16[128,384]{1,0:T(8,128)(2,1)} %bitcast.9, bf16[128,384]{1,0:T(8,128)(2,1)} %bitcast.10, bf16[128,384]{1,0:T(8,128)(2,1)} %bitcast.11, ...), custom_call_target="tpu_custom_call" | custom-call | tf_op jit(solution)/shard_map/gather_tiles/pallas_call | solution.py:484
  30.2 0.0 copy-start.1
  30.2 1.2 %copy-done.1 = bf16[16,256,128]{2,1,0:T(8,128)(2,1)S(1)} copy-done((bf16[16,256,128]{2,1,0:T(8,128)(2,1)S(1)}, bf16[16,256,128]{2,1,0:T(8,128)(2,1)}, u32[]{:S(2)}) %copy-start.1) | copy-done | bytes 1048600
  31.4 0.0 copy-start.2
  31.4 1.0 %copy-done.2 = bf16[16,128,128]{2,1,0:T(8,128)(2,1)S(1)} copy-done((bf16[16,128,128]{2,1,0:T(8,128)(2,1)S(1)}, bf16[16,128,128]{2,1,0:T(8,128)(2,1)}, u32[]{:S(2)}) %copy-start.2) | copy-done | bytes 524312
  32.5 0.0 copy-start.3
  32.5 0.7 copy-done.3
  33.2 3.7 %attention.1 = (bf16[16,128,128]{2,1,0:T(8,128)(2,1)S(1)}, f32[4,8,128]{2,1,0:T(8,128)S(1)}) custom-call(s32[16,128]{1,0:T(8,128)S(1)} %copy-done.3, bf16[16,128,128]{2,1,0:T(8,128)(2,1)S(1)} %copy-done.2, bf16[16,256,128]{2,1,0:T(8,128)(2,1)S(1)} %copy-done.1), custom_call_target="tpu_custom_call" | custom-call | tf_op jit(solution)/shard_map/attention/pallas_call | solution.py:508
  36.9 0.0 copy-start
  36.9 1.7 %copy-done = bf16[4,384,768]{2,1,0:T(8,128)(2,1)S(1)} copy-done((bf16[4,384,768]{2,1,0:T(8,128)(2,1)S(1)}, bf16[4,384,768]{2,1,0:T(8,128)(2,1)}, u32[]{:S(2)}) %copy-start) | copy-done | bytes 2359320
  38.6 46.2 %project.1 = bf16[128,384]{1,0:T(8,128)(2,1)S(1)} custom-call(bf16[16,128,128]{2,1,0:T(8,128)(2,1)S(1)} %get-tuple-element.14.o_ref, f32[4,8,128]{2,1,0:T(8,128)S(1)} %get-tuple-element.15.stat_ref, bf16[1536,768]{1,0:T(8,128)(2,1)S(1)} %bitcast.7), custom_call_target="tpu_custom_call" | custom-call | tf_op jit(solution)/shard_map/project/pallas_call | solution.py:517
  84.8 0.6 copy.9
Async XLA Ops:
  30.2 1.2 %copy-start.1 = (bf16[16,256,128]{2,1,0:T(8,128)(2,1)S(1)}, bf16[16,256,128]{2,1,0:T(8,128)(2,1)}, u32[]{:S(2)}) copy-start(bf16[16,256,128]{2,1,0:T(8,128)(2,1)} %get-tuple-element.13.kv_ref) | copy-start | bytes 3145732
  31.4 1.0 %copy-start.2 = (bf16[16,128,128]{2,1,0:T(8,128)(2,1)S(1)}, bf16[16,128,128]{2,1,0:T(8,128)(2,1)}, u32[]{:S(2)}) copy-start(bf16[16,128,128]{2,1,0:T(8,128)(2,1)} %get-tuple-element.12.q_ref) | copy-start | bytes 1572868
  32.5 0.7 copy-start.3
  36.9 1.7 %copy-start = (bf16[4,384,768]{2,1,0:T(8,128)(2,1)S(1)}, bf16[4,384,768]{2,1,0:T(8,128)(2,1)}, u32[]{:S(2)}) copy-start(bf16[4,384,768]{2,1,0:T(8,128)(2,1)} %get-tuple-element.16) | copy-start | bytes 7077892

commit v3 on v2

v3 whole, which is shorter than its diff:
```python
import functools
import math

import jax
import jax.numpy as jnp
from jax import lax
from jax.experimental import pallas as pl
from jax.experimental.pallas import tpu as pltpu
from jax.sharding import PartitionSpec as P

HD = 128
TILE = 128
NX = 4
NZ = 8
NY = 4
SLOTS = 4
ENTRIES = 2 * NZ
BF16 = jnp.bfloat16
F32 = jnp.float32
I32 = jnp.int32
EXP2_SCALE = HD ** -0.5 * math.log2(math.e)
NOTHING = -1e30
QUERIES = NX * SLOTS * TILE
MESH = pl.DeviceIdType.MESH


def head_of_row(z):
    return (3 * z + 1) // 8


def first_row(g):
    return (8 * g + 1) // 3


def last_row(g):
    return (8 * g + 9) // 3 - 1


def query_place(zq, g):
    if g == 0:
        return zq // 3, zq % 3
    if g == 1:
        return 3 + zq // 4, zq % 4
    return 7 - (7 - zq) // 3, (7 - zq) % 3


def slot_row(z, g, j):
    low = 3 * z + j
    mid = 4 * (z - 3) + j
    high = 7 - (3 * (7 - z) + j)
    row = jnp.where(g == 0, low, jnp.where(g == 1, mid, high))
    return jnp.where((j == 3) & (g != 1), -1, row)


def row_order(i, z):
    near = jnp.minimum(z, 7 - z)
    d = (i + 1) // 2
    both = z + d * (1 - 2 * (i % 2))
    return jnp.where(i <= 2 * near, both, jnp.where(z <= 3, i, 7 - i))


def remote(src, dst, send, recv, target):
    return pltpu.make_async_remote_copy(
        src_ref=src, dst_ref=dst, send_sem=send, recv_sem=recv, device_id=target, device_id_type=MESH
    )


def layer_kernel(
    counts_ref, q_ref, k_ref, v_ref, sp_ref, mp_ref, w_ref, out_ref,
    q_v, k_v, v_v, sp_v, mp_v, counts_v,
    mine, kv, qs, qt, bias, tops, totals, acc, w_v,
    o_v, stat_v, parts, part_stats, merged, full, give, got,
    z_send, z_recv, zf_send, c_send, c_recv,
    q_send, q_recv, qx_send, qx_recv, w_send, w_recv, wc_send, wc_recv,
    x_send, x_recv, s_send, s_recv, o_send, o_recv, y_send, y_recv, h_send, h_recv, local_sem,
):
    s = lax.axis_index("seq")
    p = lax.axis_index("pass")
    h = lax.axis_index("head")
    x, z = s // NZ, s % NZ
    zh, y = h // NY, h % NY
    g = head_of_row(z)
    a, b = first_row(g), last_row(g)

    def dev(seq=s, core=p, head=h):
        return {"seq": seq, "pass": core, "head": head}

    def along_x(d):
        return dev(seq=((x + d) % NX) * NZ + z)

    def along_y(d):
        return dev(head=zh * NY + (y + d) % NY)

    partner = dev(head=(1 - zh) * NY + y)
    met = (
        [dev(seq=x * NZ + (z + d) % NZ) for d in range(1, NZ)]
        + [along_x(d) for d in range(1, NX)]
        + [along_y(d) for d in range(1, NY)]
        + [dev(core=1 - p), partner]
    )
    barrier = pltpu.get_barrier_semaphore()
    for device in met:
        pl.semaphore_signal(barrier, inc=1, device_id=device, device_id_type=MESH)

    def w_cols(yy, part):
        zz = zh if part == 0 else 1 - zh
        return pl.ds(pl.multiple_of((zz * NY + yy) * (3 * HD), 3 * HD), 3 * HD)

    def part_cols(part):
        return slice(part * 3 * HD, (part + 1) * 3 * HD)

    loads = [
        pltpu.make_async_copy(src, dst, local_sem.at[i])
        for i, (src, dst) in enumerate(
            [(k_ref, k_v), (v_ref, v_v), (q_ref, q_v), (counts_ref, counts_v), (sp_ref, sp_v), (mp_ref, mp_v)]
            + [(w_ref.at[:, w_cols(y, part)], w_v.at[y, :, part_cols(part)]) for part in range(2)]
        )
    ]
    for load in loads:
        load.start()

    loads[0].wait()
    loads[1].wait()
    for n in range(3):
        cols = slice(n * HD, (n + 1) * HD)
        mine[n, :TILE, :] = k_v[:, cols]
        mine[n, TILE:, :] = v_v[:, cols].T
    kv[z] = mine[g]
    loads[2].wait()

    pl.semaphore_wait(barrier, len(met))

    def query_copies(n):
        row, slot = query_place(z, n)
        src, dst = q_v.at[:, n * HD:(n + 1) * HD], qs.at[slot * NX + x]
        away = remote(src, dst, q_send.at[n], q_recv.at[slot], dev(seq=x * NZ + row))
        here = pltpu.make_async_copy(src, dst, q_send.at[n])
        return row, away, here

    for n in range(3):
        row, away, here = query_copies(n)
        pl.when(row != z)(away.start)
        pl.when(row == z)(here.start)

    def up_copy(r, src, send):
        return remote(src, kv.at[r], send, z_recv.at[r], dev(seq=s + 1))

    def down_copy(r, src, send):
        return remote(src, kv.at[r], send, z_recv.at[r], dev(seq=s - 1))

    def entry_copy(n):
        e = jnp.maximum(first_row(n), jnp.minimum(z, last_row(n)))
        return e, remote(mine.at[n], kv.at[z], z_send.at[n], z_recv.at[z], dev(seq=x * NZ + e))

    pl.when(z < b)(up_copy(z, mine.at[g], z_send.at[3]).start)
    pl.when(z > a)(down_copy(z, mine.at[g], z_send.at[4]).start)
    for n, far in ((1, None), (0, z >= first_row(2)), (2, z <= last_row(0))):
        e, copy = entry_copy(n)
        pl.when((e != z) if far is None else (e != z) & jnp.logical_not(far))(copy.start)

    half_rows = 3 * HD // 2
    rows_mine = pl.ds(pl.multiple_of(p * half_rows, half_rows), half_rows)
    rows_other = pl.ds(pl.multiple_of((1 - p) * half_rows, half_rows), half_rows)

    def w_copy(d, part):
        return remote(
            w_ref.at[rows_mine, w_cols((y + d) % NY, part)], w_v.at[y, rows_mine, part_cols(part)],
            w_send.at[2 * d + part], w_recv.at[2 * d + part], along_y(d),
        )

    def w_arrival(d, part):
        place = w_v.at[(y + NY - d) % NY, rows_mine, part_cols(part)]
        return remote(place, place, w_send.at[2 * d + part], w_recv.at[2 * d + part], along_y(d))

    def w_swap(d, rows):
        place = w_v.at[(y + NY - d) % NY, rows]
        return remote(place, place, wc_send.at[d], wc_recv.at[d], dev(core=1 - p))

    for part in range(2):
        for d in range(1, NY):
            w_copy(d, part).start()

    for load in loads[3:6]:
        load.wait()
    slots = lax.broadcasted_iota(I32, (NX * SLOTS, 1), 0)
    tiles = jnp.full((NX * SLOTS, 1), -1, I32)
    for j in range(SLOTS):
        row = slot_row(z, g, j)
        live = (row >= 0) & (row < NZ)
        tiles = jnp.where(((slots >> 2) == j) & live, (slots & 3) * NZ + row, tiles)

    def hits(queries, keys, live_count, shift):
        live = lax.broadcasted_iota(I32, queries.shape, 1) < live_count
        row_hits = ((queries == tiles) & live).astype(F32)
        row = keys - x * NZ
        row = jnp.where((row >= 0) & (row < NZ), row + shift, -1)
        col_hits = (lax.broadcasted_iota(I32, (ENTRIES, 1), 0) == row).astype(F32)
        return lax.dot_general(col_hits, row_hits, (((1,), (1,)), ((), ())), preferred_element_type=F32)

    is_edit = (p == 1).astype(F32)
    counted = hits(sp_v[p, 0:1], sp_v[p, 1:2], counts_v[p], 0)
    counted = counted + is_edit * hits(mp_v[0:1], mp_v[1:2], counts_v[2], NZ)
    allowed = (counted > 0.5).astype(F32)
    spread = lax.broadcasted_iota(I32, (NX * SLOTS, QUERIES), 1) // TILE
    spread = (spread == lax.broadcasted_iota(I32, (NX * SLOTS, QUERIES), 0)).astype(F32)
    live = jnp.dot(allowed, spread, preferred_element_type=F32)
    bias[...] = jnp.where(live > 0.5, 0.0, NOTHING)
    tops[...] = jnp.full(tops.shape, NOTHING, F32)
    totals[...] = jnp.zeros(totals.shape, F32)
    acc[...] = jnp.zeros(acc.shape, F32)

    def chip_copy(r):
        return remote(kv.at[r], kv.at[NZ + r], c_send.at[r], c_recv.at[r], dev(core=1 - p))

    pl.when(p == 0)(chip_copy(z).start)

    def pass_on(i):
        r = row_order(i, z)
        place = kv.at[r]
        remote(place, place, z_send.at[0], z_recv.at[r], dev()).wait_recv()
        pl.when((r < z) & (z < b))(up_copy(r, place, zf_send.at[r]).start)
        pl.when((r > z) & (z > a))(down_copy(r, place, zf_send.at[r]).start)
        pl.when(p == 0)(chip_copy(r).start)

    def qx_copy(j, d):
        place = qs.at[j * NX + x]
        return remote(place, place, qx_send.at[3 * j + d - 1], qx_recv.at[3 * j + d - 1], along_x(d))

    def qx_arrival(j, d):
        place = qs.at[j * NX + (x + NX - d) % NX]
        return remote(place, place, qx_send.at[3 * j + d - 1], qx_recv.at[3 * j + d - 1], along_x(d))

    def live_slot(j):
        row = slot_row(z, g, j)
        return row, (row >= 0) & (row < NZ)

    for n in range(3):
        row, away, here = query_copies(n)
        pl.when(row == z)(here.wait)

    for j in range(SLOTS):
        row, live = live_slot(j)
        place = qs.at[j * NX + x]

        @pl.when(live)
        def _():
            pl.when(row != z)(remote(place, place, q_send.at[0], q_recv.at[j], dev()).wait_recv)
            for d in range(1, NX):
                qx_copy(j, d).start()

    pass_on(1)

    for n, near, far in ((0, 1, z >= first_row(2)), (2, 1, z <= last_row(0))):
        @pl.when(far)
        def _():
            entry_copy(near)[1].wait_send()
            entry_copy(n)[1].start()

    pass_on(2)

    for j in range(SLOTS):
        row, live = live_slot(j)

        @pl.when(live)
        def _():
            for d in range(1, NX):
                qx_arrival(j, d).wait_recv()
            for xx in range(NX):
                at = j * NX + xx
                qt[:, at * TILE:(at + 1) * TILE] = qs[at].T

    def attend(r, u, base):
        keys = jnp.concatenate([kv[base + r, :TILE, :], kv[base + u, :TILE, :]], axis=0)
        values = jnp.concatenate([kv[base + r, TILE:, :], kv[base + u, TILE:, :]], axis=1)

        def unit(i, carry):
            row, live = live_slot(i // 2)

            @pl.when(live)
            def _():
                cols = pl.ds(pl.multiple_of(i * 2 * TILE, 2 * TILE), 2 * TILE)
                scores = jnp.dot(keys, qt[:, cols], preferred_element_type=F32)
                first, second = scores[:TILE], scores[TILE:]
                first_bias = bias[pl.ds(base + r, 1), cols]
                second_bias = bias[pl.ds(base + u, 1), cols]
                top = tops[:, cols]
                new_top = jnp.maximum(top, jnp.maximum(
                    jnp.max(first, axis=0, keepdims=True) * EXP2_SCALE + first_bias,
                    jnp.max(second, axis=0, keepdims=True) * EXP2_SCALE + second_bias,
                ))
                level = jnp.maximum(new_top, NOTHING / 10)
                faded = jnp.exp2(top - new_top)
                first = jnp.exp2(first * EXP2_SCALE - (level - first_bias))
                second = jnp.exp2(second * EXP2_SCALE - (level - second_bias))
                tops[:, cols] = new_top
                totals[:, cols] = totals[:, cols] * faded + jnp.sum(
                    (first + second).reshape(16, 8, 2 * TILE), axis=0
                )
                weights = jnp.concatenate([first.astype(BF16), second.astype(BF16)], axis=0)
                acc[:, cols] = acc[:, cols] * faded + jnp.dot(values, weights, preferred_element_type=F32)

            return carry

        lax.fori_loop(0, 2 * SLOTS, unit, 0)

    def batch(i, carry):
        r, u = row_order(2 * i, z), row_order(2 * i + 1, z)

        @pl.when(i > 0)
        def _():
            pl.when(i > 1)(lambda: pass_on(2 * i))
            pass_on(2 * i + 1)

        attend(r, u, 0)

        @pl.when(p == 1)
        def _():
            chip_copy(r).wait_recv()
            chip_copy(u).wait_recv()
            attend(r, u, NZ)

        return carry

    lax.fori_loop(0, NZ // 2, batch, 0)

    whole = jnp.sum(totals[...], axis=0, keepdims=True)
    some = whole > 0.0
    inverse = 1.0 / jnp.where(some, whole, 1.0)
    level = jnp.where(some, tops[...] + jnp.log2(jnp.where(some, whole, 1.0)), NOTHING)
    for j in range(SLOTS):
        for xx in range(NX):
            at = j * NX + xx
            cols = slice(at * TILE, (at + 1) * TILE)
            stat_v[xx, j:j + 1, :] = level[:, cols]

    def stat_copy(d):
        return remote(
            stat_v.at[(x + d) % NX], part_stats.at[d - 1], s_send.at[d - 1], s_recv.at[d - 1], along_x(d)
        )

    def part_copy(j, d):
        at = 3 * j + d - 1
        return remote(
            o_v.at[j * NX + (x + d) % NX], parts.at[at], x_send.at[at], x_recv.at[at], along_x(d)
        )

    for d in range(1, NX):
        stat_copy(d).start()
    for j in range(SLOTS):
        row, live = live_slot(j)

        @pl.when(live)
        def _():
            for xx in range(NX):
                at = j * NX + xx
                cols = slice(at * TILE, (at + 1) * TILE)
                o_v[at] = (acc[:, cols] * inverse[:, cols]).astype(BF16)
            for d in range(1, NX):
                part_copy(j, d).start()

    for d in range(1, NY):
        for part in range(2):
            w_arrival(d, part).wait_recv()
        w_swap(d, rows_mine).start()

    def back(j):
        row, live = live_slot(j)
        dst = full.at[3 * y + g]
        away = remote(merged.at[j], dst, o_send.at[j], o_recv.at[g], dev(seq=x * NZ + row))
        here = pltpu.make_async_copy(merged.at[j], dst, o_send.at[j])
        return row, live, away, here

    for d in range(1, NX):
        stat_copy(d).wait_recv()
    for j in range(SLOTS):
        row, live, away, here = back(j)

        @pl.when(live)
        def _():
            stats = [stat_v[x, j:j + 1, :]] + [part_stats[d, j:j + 1, :] for d in range(3)]
            top = functools.reduce(jnp.maximum, stats)
            shares = [jnp.exp2(stat - top) for stat in stats]
            share_sum = sum(shares)
            for d in range(1, NX):
                part_copy(j, d).wait_recv()
            blocks = [o_v[j * NX + x]] + [parts[3 * j + d] for d in range(3)]
            mixed = sum(block.astype(F32) * (share / share_sum) for block, share in zip(blocks, shares))
            merged[j] = mixed.T.astype(BF16)
            pl.when(row != z)(away.start)
            pl.when(row == z)(here.start)

    def y_copy(n, d):
        block = full.at[3 * y + n]
        return remote(block, block, y_send.at[3 * n + d - 1], y_recv.at[3 * n + d - 1], along_y(d))

    def y_arrival(n, d):
        block = full.at[3 * ((y + NY - d) % NY) + n]
        return remote(block, block, y_send.at[3 * n + d - 1], y_recv.at[3 * n + d - 1], along_y(d))

    for j in range(SLOTS):
        row, live, away, here = back(j)
        pl.when(live & (row == z))(here.wait)

    for n in range(3):
        row, _slot = query_place(z, n)
        block = full.at[3 * y + n]
        pl.when(row != z)(remote(block, block, o_send.at[0], o_recv.at[n], dev()).wait_recv)
        for d in range(1, NY):
            y_copy(n, d).start()

    for load in loads[6:]:
        load.wait()
    for d in range(1, NY):
        w_swap(d, rows_other).wait_recv()
    for n in range(3):
        for d in range(1, NY):
            y_arrival(n, d).wait_recv()

    def projected(part):
        total = jnp.zeros((TILE, 3 * HD), F32)
        for n in range(3 * NY):
            weights = w_v[n // 3, n % 3 * HD:(n % 3 + 1) * HD, part_cols(part)]
            total = total + jnp.dot(full[n], weights, preferred_element_type=F32)
        return total

    give[...] = projected(1).astype(BF16)
    swap = remote(give, got, h_send, h_recv, partner)
    swap.start()
    own = projected(0)
    swap.wait_recv()
    out_ref[...] = (own + got[...].astype(F32)).astype(BF16)

    def drain(r, carry):
        place = kv.at[r]
        pl.when((r < z) & (z < b))(up_copy(r, place, zf_send.at[r]).wait_send)
        pl.when((r > z) & (z > a))(down_copy(r, place, zf_send.at[r]).wait_send)
        pl.when(p == 0)(chip_copy(r).wait_send)
        return carry

    lax.fori_loop(0, NZ, drain, 0)
    pl.when(z < b)(up_copy(z, mine.at[g], z_send.at[3]).wait_send)
    pl.when(z > a)(down_copy(z, mine.at[g], z_send.at[4]).wait_send)
    middle = (z > last_row(0)) & (z < first_row(2))
    for n in range(3):
        e, copy = entry_copy(n)
        pl.when(((e != z) & middle) if n == 1 else (e != z))(copy.wait_send)
        row, away, here = query_copies(n)
        pl.when(row != z)(away.wait_send)

    for j in range(SLOTS):
        row, live, away, here = back(j)

        @pl.when(live)
        def _():
            for d in range(1, NX):
                qx_copy(j, d).wait_send()
                part_copy(j, d).wait_send()
            pl.when(row != z)(away.wait_send)

    for d in range(1, NX):
        stat_copy(d).wait_send()
    for d in range(1, NY):
        for part in range(2):
            w_copy(d, part).wait_send()
        w_swap(d, rows_mine).wait_send()
        for n in range(3):
            y_copy(n, d).wait_send()
    swap.wait_send()


def on_device(queries, keys, values, self_pairs, mask_pairs, counts, out_weight):
    hbm = pl.BlockSpec(memory_space=pltpu.HBM)
    vmem = pltpu.VMEM
    dma = pltpu.SemaphoreType.DMA
    rows = (TILE, 3 * HD)
    projected = pl.pallas_call(
        layer_kernel,
        out_shape=jax.ShapeDtypeStruct(rows, BF16),
        in_specs=[hbm] * 7,
        out_specs=pl.BlockSpec(memory_space=vmem),
        scratch_shapes=[
            vmem(rows, BF16), vmem(rows, BF16), vmem(rows, BF16),
            vmem((2, 2, self_pairs.shape[1]), I32), vmem((2, mask_pairs.shape[0]), I32), pltpu.SMEM((3,), I32),
            vmem((3, 2 * TILE, HD), BF16),
            vmem((ENTRIES, 2 * TILE, HD), BF16),
            vmem((NX * SLOTS, TILE, HD), BF16),
            vmem((HD, QUERIES), BF16),
            vmem((ENTRIES, QUERIES), F32),
            vmem((1, QUERIES), F32),
            vmem((8, QUERIES), F32),
            vmem((HD, QUERIES), F32),
            vmem((NY, 3 * HD, 6 * HD), BF16),
            vmem((NX * SLOTS, HD, TILE), BF16),
            vmem((NX, 8, TILE), F32),
            vmem((3 * SLOTS, HD, TILE), BF16),
            vmem((3, 8, TILE), F32),
            vmem((SLOTS, TILE, HD), BF16),
            vmem((3 * NY, TILE, HD), BF16),
            vmem(rows, BF16), vmem(rows, BF16),
            dma((5,)), dma((NZ,)), dma((NZ,)), dma((NZ,)), dma((NZ,)),
            dma((3,)), dma((SLOTS,)), dma((3 * SLOTS,)), dma((3 * SLOTS,)),
            dma((2 * NY,)), dma((2 * NY,)), dma((NY,)), dma((NY,)),
            dma((3 * SLOTS,)), dma((3 * SLOTS,)), dma((3,)), dma((3,)),
            dma((SLOTS,)), dma((3,)), dma((9,)), dma((9,)), dma, dma, dma((8,)),
        ],
        compiler_params=pltpu.CompilerParams(
            collective_id=0, has_side_effects=True, vmem_limit_bytes=60 * 1024 * 1024
        ),
        name="layer",
    )(
        counts, queries[0], keys[0], values[0],
        jnp.swapaxes(self_pairs, 1, 2), jnp.swapaxes(mask_pairs, 0, 1), out_weight,
    )
    return projected[None]


def solution(mesh):
    in_specs = (
        P("pass", "seq", "head"),
        P("pass", "seq", "head"),
        P("pass", "seq", "head"),
        P(),
        P(),
        P(),
        P("head", None),
    )
    out_specs = P("pass", "seq", "head")
    return jax.shard_map(
        on_device, mesh=mesh, in_specs=in_specs, out_specs=out_specs, check_vma=False
    )
```

time: 85.7 us -> 81.3 us (0.949)
  the two profiles are of different devices: /device:TPU:70 before, /device:TPU:21 now
where the time goes in v3:
time: 81.3 us; the launch traced here: 81.1 us
  Pallas kernels  79.6 us (98%)
  local copies, waits for them, and re-layouts  1.54 us (2%)
    pallas_call x1, Pallas kernels, on_device(): pl.pallas_call(layer_kernel, out_shape=jax.ShapeDtypeStruct(rows, BF16),...  79.6 us

profile of v3, /device:TPU:21, one launch (start us, length us, event | category | flops | bytes accessed | tf_op | source)
XLA Modules:
  0.0 81.1 jit_solution(3367098362492532521)
XLA Ops:
  0.0 79.6 %layer.1 = bf16[128,384]{1,0:T(8,128)(2,1)} custom-call(s32[3]{0:T(128)} %counts_ref.1, bf16[128,384]{1,0:T(8,128)(2,1)} %bitcast.7, bf16[128,384]{1,0:T(8,128)(2,1)} %bitcast.8, bf16[128,384]{1,0:T(8,128)(2,1)} %bitcast.9, s32[2,2,160]{2,1,0:T(2,128)} %bitcast.10, s32[2,128]{1,0:T(2,128)} %bitcast.11, bf16[384,3072]{1,0:T(8,128)(2,1)} %w_ref.1), custom_call_target="tpu_custom_call" | custom-call | tf_op jit(solution)/shard_map/layer/pallas_call | solution.py:476
  79.6 1.5 %copy.9 = bf16[1,128,384]{2,1,0:T(8,128)(2,1)} copy(bf16[1,128,384]{2,1,0:T(8,128)(2,1)} %bitcast.6) | data formatting | bytes 196608

commit v4 on v3

--- a/solution.py
+++ b/solution.py
@@ -72,7 +72,7 @@
     o_v, stat_v, parts, part_stats, merged, full, give, got,
     z_send, z_recv, zf_send, c_send, c_recv,
     q_send, q_recv, qx_send, qx_recv, w_send, w_recv, wc_send, wc_recv,
-    x_send, x_recv, s_send, s_recv, o_send, o_recv, y_send, y_recv, h_send, h_recv, local_sem,
+    x_send, x_recv, s_send, s_recv, o_send, o_recv, y_send, y_recv, h_send, h_recv, turn, local_sem,
 ):
     s = lax.axis_index("seq")
     p = lax.axis_index("pass")
@@ -154,9 +154,12 @@
 
     pl.when(z < b)(up_copy(z, mine.at[g], z_send.at[3]).start)
     pl.when(z > a)(down_copy(z, mine.at[g], z_send.at[4]).start)
-    for n, far in ((1, None), (0, z >= first_row(2)), (2, z <= last_row(0))):
+    def later(e):
+        return (p == 1) & ((e - z) * (e - z) > 1)
+
+    for n in range(3):
         e, copy = entry_copy(n)
-        pl.when((e != z) if far is None else (e != z) & jnp.logical_not(far))(copy.start)
+        pl.when((e != z) & jnp.logical_not(later(e)))(copy.start)
 
     half_rows = 3 * HD // 2
     rows_mine = pl.ds(pl.multiple_of(p * half_rows, half_rows), half_rows)
@@ -250,13 +253,27 @@
 
     pass_on(1)
 
-    for n, near, far in ((0, 1, z >= first_row(2)), (2, 1, z <= last_row(0))):
-        @pl.when(far)
-        def _():
-            entry_copy(near)[1].wait_send()
-            entry_copy(n)[1].start()
-
     pass_on(2)
+
+    @pl.when(p == 0)
+    def _():
+        for n in range(3):
+            e, copy = entry_copy(n)
+            pl.when(e != z)(copy.wait_send)
+        pl.semaphore_signal(turn, inc=1, device_id=dev(core=1), device_id_type=MESH)
+
+        def passing(i, carry):
+            pass_on(i)
+            return carry
+
+        lax.fori_loop(3, NZ, passing, 0)
+
+    @pl.when(p == 1)
+    def _():
+        pl.semaphore_wait(turn, 1)
+        for n in range(3):
+            e, copy = entry_copy(n)
+            pl.when(later(e))(copy.start)
 
     for j in range(SLOTS):
         row, live = live_slot(j)
@@ -269,59 +286,57 @@
                 at = j * NX + xx
                 qt[:, at * TILE:(at + 1) * TILE] = qs[at].T
 
+    live_slots = jnp.where(g == 1, 4, jnp.where((z == 2) | (z == 5), 2, 3))
+
     def attend(r, u, base):
+        for width in range(2, SLOTS + 1):
+            pl.when(live_slots == width)(functools.partial(attend_slots, r, u, base, width * NX * TILE))
+
+    def attend_slots(r, u, base, width):
+        cols = slice(0, width)
         keys = jnp.concatenate([kv[base + r, :TILE, :], kv[base + u, :TILE, :]], axis=0)
         values = jnp.concatenate([kv[base + r, TILE:, :], kv[base + u, TILE:, :]], axis=1)
-
-        def unit(i, carry):
-            row, live = live_slot(i // 2)
-
-            @pl.when(live)
-            def _():
-                cols = pl.ds(pl.multiple_of(i * 2 * TILE, 2 * TILE), 2 * TILE)
-                scores = jnp.dot(keys, qt[:, cols], preferred_element_type=F32)
-                first, second = scores[:TILE], scores[TILE:]
-                first_bias = bias[pl.ds(base + r, 1), cols]
-                second_bias = bias[pl.ds(base + u, 1), cols]
-                top = tops[:, cols]
-                new_top = jnp.maximum(top, jnp.maximum(
-                    jnp.max(first, axis=0, keepdims=True) * EXP2_SCALE + first_bias,
-                    jnp.max(second, axis=0, keepdims=True) * EXP2_SCALE + second_bias,
-                ))
-                level = jnp.maximum(new_top, NOTHING / 10)
-                faded = jnp.exp2(top - new_top)
-                first = jnp.exp2(first * EXP2_SCALE - (level - first_bias))
-                second = jnp.exp2(second * EXP2_SCALE - (level - second_bias))
-                tops[:, cols] = new_top
-                totals[:, cols] = totals[:, cols] * faded + jnp.sum(
-                    (first + second).reshape(16, 8, 2 * TILE), axis=0
-                )
-                weights = jnp.concatenate([first.astype(BF16), second.astype(BF16)], axis=0)
-                acc[:, cols] = acc[:, cols] * faded + jnp.dot(values, weights, preferred_element_type=F32)
-
-            return carry
-
-        lax.fori_loop(0, 2 * SLOTS, unit, 0)
-
-    def batch(i, carry):
-        r, u = row_order(2 * i, z), row_order(2 * i + 1, z)
-
-        @pl.when(i > 0)
-        def _():
-            pl.when(i > 1)(lambda: pass_on(2 * i))
-            pass_on(2 * i + 1)
-
-        attend(r, u, 0)
-
-        @pl.when(p == 1)
+        scores = jnp.dot(keys, qt[:, cols], preferred_element_type=F32)
+        first, second = scores[:TILE], scores[TILE:]
+        first_bias = bias[pl.ds(base + r, 1), cols]
+        second_bias = bias[pl.ds(base + u, 1), cols]
+        top = tops[:, cols]
+        new_top = jnp.maximum(top, jnp.maximum(
+            jnp.max(first, axis=0, keepdims=True) * EXP2_SCALE + first_bias,
+            jnp.max(second, axis=0, keepdims=True) * EXP2_SCALE + second_bias,
+        ))
+        level = jnp.maximum(new_top, NOTHING / 10)
+        faded = jnp.exp2(top - new_top)
+        first = jnp.exp2(first * EXP2_SCALE - (level - first_bias))
+        second = jnp.exp2(second * EXP2_SCALE - (level - second_bias))
+        tops[:, cols] = new_top
+        totals[:, cols] = totals[:, cols] * faded + jnp.sum((first + second).reshape(16, 8, width), axis=0)
+        weights = jnp.concatenate([first.astype(BF16), second.astype(BF16)], axis=0)
+        acc[:, cols] = acc[:, cols] * faded + jnp.dot(values, weights, preferred_element_type=F32)
+
+    def step(i, carry):
+        cross = (i != 1) & (i < 5)
+        at = jnp.where(i < 2, 0, jnp.where(i < 5, i - 1, i - 4))
+        r, u = row_order(2 * at, z), row_order(2 * at + 1, z)
+
+        @pl.when(cross & (p == 1))
         def _():
             chip_copy(r).wait_recv()
             chip_copy(u).wait_recv()
             attend(r, u, NZ)
 
+        @pl.when(jnp.logical_not(cross))
+        def _():
+            @pl.when((at > 0) & (p == 1))
+            def _():
+                pl.when(at > 1)(lambda: pass_on(2 * at))
+                pass_on(2 * at + 1)
+
+            attend(r, u, 0)
+
         return carry
 
-    lax.fori_loop(0, NZ // 2, batch, 0)
+    lax.fori_loop(0, NZ, step, 0)
 
     whole = jnp.sum(totals[...], axis=0, keepdims=True)
     some = whole > 0.0
@@ -440,10 +455,9 @@
     lax.fori_loop(0, NZ, drain, 0)
     pl.when(z < b)(up_copy(z, mine.at[g], z_send.at[3]).wait_send)
     pl.when(z > a)(down_copy(z, mine.at[g], z_send.at[4]).wait_send)
-    middle = (z > last_row(0)) & (z < first_row(2))
     for n in range(3):
         e, copy = entry_copy(n)
-        pl.when(((e != z) & middle) if n == 1 else (e != z))(copy.wait_send)
+        pl.when((e != z) & (p == 1))(copy.wait_send)
         row, away, here = query_copies(n)
         pl.when(row != z)(away.wait_send)
 
@@ -501,7 +515,7 @@
             dma((3,)), dma((SLOTS,)), dma((3 * SLOTS,)), dma((3 * SLOTS,)),
             dma((2 * NY,)), dma((2 * NY,)), dma((NY,)), dma((NY,)),
             dma((3 * SLOTS,)), dma((3 * SLOTS,)), dma((3,)), dma((3,)),
-            dma((SLOTS,)), dma((3,)), dma((9,)), dma((9,)), dma, dma, dma((8,)),
+            dma((SLOTS,)), dma((3,)), dma((9,)), dma((9,)), dma, dma, pltpu.SemaphoreType.REGULAR, dma((8,)),
         ],
         compiler_params=pltpu.CompilerParams(
             collective_id=0, has_side_effects=True, vmem_limit_bytes=60 * 1024 * 1024

time: 81.3 us -> 71.8 us (0.88)
  the two profiles are of different devices: /device:TPU:21 before, /device:TPU:65 now
where the time goes in v4:
time: 71.8 us; the launch traced here: 71.5 us
  Pallas kernels  70 us (97%)
  local copies, waits for them, and re-layouts  1.54 us (2%)
    pallas_call x1, Pallas kernels, on_device(): pl.pallas_call(layer_kernel, out_shape=jax.ShapeDtypeStruct(rows, BF16),...  70 us
    unnamed x1, local copies, waits for them, and re-layouts  1.54 us

profile of v4, /device:TPU:65, one launch (start us, length us, event | category | flops | bytes accessed | tf_op | source)
XLA Modules:
  0.0 71.5 jit_solution(1864771735140193921)
XLA Ops:
  0.0 70.0 %layer.1 = bf16[128,384]{1,0:T(8,128)(2,1)} custom-call(s32[3]{0:T(128)} %counts_ref.1, bf16[128,384]{1,0:T(8,128)(2,1)} %bitcast.7, bf16[128,384]{1,0:T(8,128)(2,1)} %bitcast.8, bf16[128,384]{1,0:T(8,128)(2,1)} %bitcast.9, s32[2,2,160]{2,1,0:T(2,128)} %bitcast.10, s32[2,128]{1,0:T(2,128)} %bitcast.11, bf16[384,3072]{1,0:T(8,128)(2,1)} %w_ref.1), custom_call_target="tpu_custom_call" | custom-call | tf_op jit(solution)/shard_map/layer/pallas_call | solution.py:490
  70.0 1.5 %copy.9 = bf16[1,128,384]{2,1,0:T(8,128)(2,1)} copy(bf16[1,128,384]{2,1,0:T(8,128)(2,1)} %bitcast.6) | data formatting | bytes 196608

commit v5 on v4

--- a/solution.py
+++ b/solution.py
@@ -248,7 +248,7 @@
         @pl.when(live)
         def _():
             pl.when(row != z)(remote(place, place, q_send.at[0], q_recv.at[j], dev()).wait_recv)
-            for d in range(1, NX):
+            for d in (2, 1, 3):
                 qx_copy(j, d).start()
 
     pass_on(1)
@@ -257,9 +257,8 @@
 
     @pl.when(p == 0)
     def _():
-        for n in range(3):
-            e, copy = entry_copy(n)
-            pl.when(e != z)(copy.wait_send)
+        for n in range(2):
+            pl.when((g == 1) == (n == 0))(entry_copy(n)[1].wait_send)
         pl.semaphore_signal(turn, inc=1, device_id=dev(core=1), device_id_type=MESH)
 
         def passing(i, carry):
@@ -370,7 +369,7 @@
                 at = j * NX + xx
                 cols = slice(at * TILE, (at + 1) * TILE)
                 o_v[at] = (acc[:, cols] * inverse[:, cols]).astype(BF16)
-            for d in range(1, NX):
+            for d in (2, 1, 3):
                 part_copy(j, d).start()
 
     for d in range(1, NY):
@@ -420,28 +419,28 @@
         row, _slot = query_place(z, n)
         block = full.at[3 * y + n]
         pl.when(row != z)(remote(block, block, o_send.at[0], o_recv.at[n], dev()).wait_recv)
-        for d in range(1, NY):
+        for d in (2, 1, 3):
             y_copy(n, d).start()
 
     for load in loads[6:]:
         load.wait()
     for d in range(1, NY):
         w_swap(d, rows_other).wait_recv()
+    def projected(n, d, part):
+        at = (y + NY - d) % NY
+        return jnp.dot(
+            full[3 * at + n], w_v[at, n * HD:(n + 1) * HD, part_cols(part)], preferred_element_type=F32
+        )
+
+    theirs = sum(projected(n, 0, 1) for n in range(3))
     for n in range(3):
         for d in range(1, NY):
             y_arrival(n, d).wait_recv()
-
-    def projected(part):
-        total = jnp.zeros((TILE, 3 * HD), F32)
-        for n in range(3 * NY):
-            weights = w_v[n // 3, n % 3 * HD:(n % 3 + 1) * HD, part_cols(part)]
-            total = total + jnp.dot(full[n], weights, preferred_element_type=F32)
-        return total
-
-    give[...] = projected(1).astype(BF16)
+            theirs = theirs + projected(n, d, 1)
+    give[...] = theirs.astype(BF16)
     swap = remote(give, got, h_send, h_recv, partner)
     swap.start()
-    own = projected(0)
+    own = sum(projected(n, d, 0) for n in range(3) for d in range(NY))
     swap.wait_recv()
     out_ref[...] = (own + got[...].astype(F32)).astype(BF16)
 
@@ -457,7 +456,8 @@
     pl.when(z > a)(down_copy(z, mine.at[g], z_send.at[4]).wait_send)
     for n in range(3):
         e, copy = entry_copy(n)
-        pl.when((e != z) & (p == 1))(copy.wait_send)
+        waited = (p == 0) & ((g == 1) if n == 0 else (g != 1) & (n == 1))
+        pl.when((e != z) & jnp.logical_not(waited))(copy.wait_send)
         row, away, here = query_copies(n)
         pl.when(row != z)(away.wait_send)
 
@@ -518,13 +518,16 @@
             dma((SLOTS,)), dma((3,)), dma((9,)), dma((9,)), dma, dma, pltpu.SemaphoreType.REGULAR, dma((8,)),
         ],
         compiler_params=pltpu.CompilerParams(
-            collective_id=0, has_side_effects=True, vmem_limit_bytes=60 * 1024 * 1024
+            collective_id=0, has_side_effects=True, vmem_limit_bytes=32 * 1024 * 1024
         ),
         name="layer",
-    )(
-        counts, queries[0], keys[0], values[0],
-        jnp.swapaxes(self_pairs, 1, 2), jnp.swapaxes(mask_pairs, 0, 1), out_weight,
-    )
+    )(*[
+        pltpu.with_memory_space_constraint(each, pltpu.HBM)
+        for each in (
+            counts, queries[0], keys[0], values[0],
+            jnp.swapaxes(self_pairs, 1, 2), jnp.swapaxes(mask_pairs, 0, 1), out_weight,
+        )
+    ])
     return projected[None]
 
 

time: 71.8 us -> 69.9 us (0.974)
  the two profiles are of different devices: /device:TPU:65 before, /device:TPU:67 now
where the time goes in v5:
time: 69.9 us; the launch traced here: 69.7 us
  Pallas kernels  69.1 us (99%)
    pallas_call x1, Pallas kernels, on_device(): pl.pallas_call(layer_kernel, out_shape=jax.ShapeDtypeStruct(rows, BF16),...  69.1 us

profile of v5, /device:TPU:67, one launch (start us, length us, event | category | flops | bytes accessed | tf_op | source)
XLA Modules:
  0.0 69.7 jit_solution(5890779244134780453)
XLA Ops:
  0.0 69.1 %layer.1 = bf16[128,384]{1,0:T(8,128)(2,1)S(1)} custom-call(s32[3]{0:T(128)} %counts_ref.1, bf16[128,384]{1,0:T(8,128)(2,1)} %bitcast.7, bf16[128,384]{1,0:T(8,128)(2,1)} %bitcast.8, bf16[128,384]{1,0:T(8,128)(2,1)} %bitcast.9, s32[2,2,160]{2,1,0:T(2,128)} %bitcast.10, s32[2,128]{1,0:T(2,128)} %bitcast.11, bf16[384,3072]{1,0:T(8,128)(2,1)} %w_ref.1), custom_call_target="tpu_custom_call" | custom-call | tf_op jit(solution)/shard_map/layer/pallas_call | solution.py:490
  69.1 0.6 copy.9

commit v6 on v5

--- a/solution.py
+++ b/solution.py
@@ -63,6 +63,19 @@
     return pltpu.make_async_remote_copy(
         src_ref=src, dst_ref=dst, send_sem=send, recv_sem=recv, device_id=target, device_id_type=MESH
     )
+
+
+class Copies:
+    def __init__(self, copies):
+        self.copies = copies
+
+    def start(self):
+        for copy in self.copies:
+            copy.start()
+
+    def wait_send(self):
+        for copy in self.copies:
+            copy.wait_send()
 
 
 def layer_kernel(
@@ -142,18 +155,24 @@
         pl.when(row != z)(away.start)
         pl.when(row == z)(here.start)
 
-    def up_copy(r, src, send):
-        return remote(src, kv.at[r], send, z_recv.at[r], dev(seq=s + 1))
-
-    def down_copy(r, src, send):
-        return remote(src, kv.at[r], send, z_recv.at[r], dev(seq=s - 1))
+    def two_copies(r, src, sems, at, target):
+        return Copies([
+            remote(src.at[part], kv.at[r].at[part], sems.at[2 * at + k], z_recv.at[2 * r + k], target)
+            for k, part in enumerate((slice(0, TILE), slice(TILE, 2 * TILE)))
+        ])
+
+    def up_copy(r, src, sems, at):
+        return two_copies(r, src, sems, at, dev(seq=s + 1))
+
+    def down_copy(r, src, sems, at):
+        return two_copies(r, src, sems, at, dev(seq=s - 1))
 
     def entry_copy(n):
         e = jnp.maximum(first_row(n), jnp.minimum(z, last_row(n)))
-        return e, remote(mine.at[n], kv.at[z], z_send.at[n], z_recv.at[z], dev(seq=x * NZ + e))
-
-    pl.when(z < b)(up_copy(z, mine.at[g], z_send.at[3]).start)
-    pl.when(z > a)(down_copy(z, mine.at[g], z_send.at[4]).start)
+        return e, two_copies(z, mine.at[n], z_send, n, dev(seq=x * NZ + e))
+
+    pl.when(z < b)(up_copy(z, mine.at[g], z_send, 3).start)
+    pl.when(z > a)(down_copy(z, mine.at[g], z_send, 4).start)
     def later(e):
         return (p == 1) & ((e - z) * (e - z) > 1)
 
@@ -220,9 +239,12 @@
     def pass_on(i):
         r = row_order(i, z)
         place = kv.at[r]
-        remote(place, place, z_send.at[0], z_recv.at[r], dev()).wait_recv()
-        pl.when((r < z) & (z < b))(up_copy(r, place, zf_send.at[r]).start)
-        pl.when((r > z) & (z > a))(down_copy(r, place, zf_send.at[r]).start)
+        arriving = two_copies(r, place, z_send, 0, dev())
+        up, down = up_copy(r, place, zf_send, r), down_copy(r, place, zf_send, r)
+        for k in range(2):
+            arriving.copies[k].wait_recv()
+            pl.when((r < z) & (z < b))(up.copies[k].start)
+            pl.when((r > z) & (z > a))(down.copies[k].start)
         pl.when(p == 0)(chip_copy(r).start)
 
     def qx_copy(j, d):
@@ -446,14 +468,14 @@
 
     def drain(r, carry):
         place = kv.at[r]
-        pl.when((r < z) & (z < b))(up_copy(r, place, zf_send.at[r]).wait_send)
-        pl.when((r > z) & (z > a))(down_copy(r, place, zf_send.at[r]).wait_send)
+        pl.when((r < z) & (z < b))(up_copy(r, place, zf_send, r).wait_send)
+        pl.when((r > z) & (z > a))(down_copy(r, place, zf_send, r).wait_send)
         pl.when(p == 0)(chip_copy(r).wait_send)
         return carry
 
     lax.fori_loop(0, NZ, drain, 0)
-    pl.when(z < b)(up_copy(z, mine.at[g], z_send.at[3]).wait_send)
-    pl.when(z > a)(down_copy(z, mine.at[g], z_send.at[4]).wait_send)
+    pl.when(z < b)(up_copy(z, mine.at[g], z_send, 3).wait_send)
+    pl.when(z > a)(down_copy(z, mine.at[g], z_send, 4).wait_send)
     for n in range(3):
         e, copy = entry_copy(n)
         waited = (p == 0) & ((g == 1) if n == 0 else (g != 1) & (n == 1))
@@ -511,7 +533,7 @@
             vmem((SLOTS, TILE, HD), BF16),
             vmem((3 * NY, TILE, HD), BF16),
             vmem(rows, BF16), vmem(rows, BF16),
-            dma((5,)), dma((NZ,)), dma((NZ,)), dma((NZ,)), dma((NZ,)),
+            dma((10,)), dma((2 * NZ,)), dma((2 * NZ,)), dma((NZ,)), dma((NZ,)),
             dma((3,)), dma((SLOTS,)), dma((3 * SLOTS,)), dma((3 * SLOTS,)),
             dma((2 * NY,)), dma((2 * NY,)), dma((NY,)), dma((NY,)),
             dma((3 * SLOTS,)), dma((3 * SLOTS,)), dma((3,)), dma((3,)),

time: 69.9 us -> 69.1 us (0.989)
  the two profiles are of different devices: /device:TPU:67 before, /device:TPU:65 now
where the time goes in v6:
time: 69.1 us; the launch traced here: 68.9 us
  Pallas kernels  68.3 us (99%)
    pallas_call x1, Pallas kernels, on_device(): pl.pallas_call(layer_kernel, out_shape=jax.ShapeDtypeStruct(rows, BF16),...  68.3 us

profile of v6, /device:TPU:65, one launch (start us, length us, event | category | flops | bytes accessed | tf_op | source)
XLA Modules:
  0.0 68.9 jit_solution(11290177793688458067)
XLA Ops:
  0.0 68.3 %layer.1 = bf16[128,384]{1,0:T(8,128)(2,1)S(1)} custom-call(s32[3]{0:T(128)} %counts_ref.1, bf16[128,384]{1,0:T(8,128)(2,1)} %bitcast.7, bf16[128,384]{1,0:T(8,128)(2,1)} %bitcast.8, bf16[128,384]{1,0:T(8,128)(2,1)} %bitcast.9, s32[2,2,160]{2,1,0:T(2,128)} %bitcast.10, s32[2,128]{1,0:T(2,128)} %bitcast.11, bf16[384,3072]{1,0:T(8,128)(2,1)} %w_ref.1), custom_call_target="tpu_custom_call" | custom-call | tf_op jit(solution)/shard_map/layer/pallas_call | solution.py:512
  68.3 0.6 copy.9

commit v7 on v6

--- a/solution.py
+++ b/solution.py
@@ -344,17 +344,13 @@
         def _():
             chip_copy(r).wait_recv()
             chip_copy(u).wait_recv()
-            attend(r, u, NZ)
-
-        @pl.when(jnp.logical_not(cross))
-        def _():
-            @pl.when((at > 0) & (p == 1))
-            def _():
-                pl.when(at > 1)(lambda: pass_on(2 * at))
-                pass_on(2 * at + 1)
-
-            attend(r, u, 0)
-
+
+        @pl.when(jnp.logical_not(cross) & (at > 0) & (p == 1))
+        def _():
+            pl.when(at > 1)(lambda: pass_on(2 * at))
+            pass_on(2 * at + 1)
+
+        pl.when(jnp.logical_not(cross) | (p == 1))(lambda: attend(r, u, jnp.where(cross, NZ, 0)))
         return carry
 
     lax.fori_loop(0, NZ, step, 0)
@@ -403,13 +399,12 @@
         row, live = live_slot(j)
         dst = full.at[3 * y + g]
         away = remote(merged.at[j], dst, o_send.at[j], o_recv.at[g], dev(seq=x * NZ + row))
-        here = pltpu.make_async_copy(merged.at[j], dst, o_send.at[j])
-        return row, live, away, here
+        return row, live, away
 
     for d in range(1, NX):
         stat_copy(d).wait_recv()
     for j in range(SLOTS):
-        row, live, away, here = back(j)
+        row, live, away = back(j)
 
         @pl.when(live)
         def _():
@@ -421,9 +416,16 @@
                 part_copy(j, d).wait_recv()
             blocks = [o_v[j * NX + x]] + [parts[3 * j + d] for d in range(3)]
             mixed = sum(block.astype(F32) * (share / share_sum) for block, share in zip(blocks, shares))
-            merged[j] = mixed.T.astype(BF16)
-            pl.when(row != z)(away.start)
-            pl.when(row == z)(here.start)
+            tile = mixed.T.astype(BF16)
+
+            @pl.when(row == z)
+            def _():
+                full[3 * y + g] = tile
+
+            @pl.when(row != z)
+            def _():
+                merged[j] = tile
+                away.start()
 
     def y_copy(n, d):
         block = full.at[3 * y + n]
@@ -432,10 +434,6 @@
     def y_arrival(n, d):
         block = full.at[3 * ((y + NY - d) % NY) + n]
         return remote(block, block, y_send.at[3 * n + d - 1], y_recv.at[3 * n + d - 1], along_y(d))
-
-    for j in range(SLOTS):
-        row, live, away, here = back(j)
-        pl.when(live & (row == z))(here.wait)
 
     for n in range(3):
         row, _slot = query_place(z, n)
@@ -484,7 +482,7 @@
         pl.when(row != z)(away.wait_send)
 
     for j in range(SLOTS):
-        row, live, away, here = back(j)
+        row, live, away = back(j)
 
         @pl.when(live)
         def _():

time: 69.1 us -> 69 us (level)
  no operation moved by 1% of the time
where the time goes in v7:
time: 69 us; the launch traced here: 68.8 us
  Pallas kernels  68.2 us (99%)
    pallas_call x1, Pallas kernels, on_device(): pl.pallas_call(layer_kernel, out_shape=jax.ShapeDtypeStruct(rows, BF16),...  68.2 us

profile of v7, /device:TPU:65, one launch (start us, length us, event | category | flops | bytes accessed | tf_op | source)
XLA Modules:
  0.0 68.8 jit_solution(5166156474548979673)
XLA Ops:
  0.0 68.2 %layer.1 = bf16[128,384]{1,0:T(8,128)(2,1)S(1)} custom-call(s32[3]{0:T(128)} %counts_ref.1, bf16[128,384]{1,0:T(8,128)(2,1)} %bitcast.7, bf16[128,384]{1,0:T(8,128)(2,1)} %bitcast.8, bf16[128,384]{1,0:T(8,128)(2,1)} %bitcast.9, s32[2,2,160]{2,1,0:T(2,128)} %bitcast.10, s32[2,128]{1,0:T(2,128)} %bitcast.11, bf16[384,3072]{1,0:T(8,128)(2,1)} %w_ref.1), custom_call_target="tpu_custom_call" | custom-call | tf_op jit(solution)/shard_map/layer/pallas_call | solution.py:510
  68.2 0.6 copy.9
